TPU v7x, 32 devices: a whole 2x2x4 slice. The times are simulated.
32 devices in a mesh: seq: 8 (over y, x, core), fsdp: 4 (over z).
Axes of the slice: x: 2, y: 2, z: 4, core: 2. Of those that a mesh axis runs over, the one named last changes fastest.
Arguments:
- frames: bfloat16 [4, 1024, 1024], P('fsdp', 'seq'), may hold values from -6 to 6
- lengths: int32 [4, 4], P('fsdp'), may hold values from 1 to 897, as said below
- up_first: bfloat16 [1024, 4096], P('fsdp'), may hold values from -0.1875 to 0.1875
- down_first: bfloat16 [4096, 1024], P('fsdp'), may hold values from -0.09375 to 0.09375
- joint_qkv: bfloat16 [1024, 3072], P('fsdp'), may hold values from -0.1875 to 0.1875
- attn_out: bfloat16 [1024, 1024], P('fsdp'), may hold values from -0.75 to 0.75
- conv_in: bfloat16 [1024, 2048], P('fsdp'), may hold values from -0.1875 to 0.1875
- conv_kernel: bfloat16 [5, 1024], P(None, 'fsdp'), may hold values from -2.5 to 2.5
- batch_gain: bfloat16 [1024], P('fsdp'), may hold values from 0.5 to 1.5
- conv_out: bfloat16 [1024, 1024], P('fsdp'), may hold values from -0.1875 to 0.1875
- up_second: bfloat16 [1024, 4096], P('fsdp'), may hold values from -0.1875 to 0.1875
- down_second: bfloat16 [4096, 1024], P('fsdp'), may hold values from -0.09375 to 0.09375
- norm_gains: bfloat16 [5, 1024], P(None, 'fsdp'), may hold values from 0.5 to 1.5
- slopes: float32 [8], replicated, may hold values from 0.0005 to 0.05
- out_grad: bfloat16 [4, 1024, 1024], P('fsdp', 'seq'), may hold values from -6 to 6
Outputs:
- output: bfloat16 [4, 1024, 1024], P('fsdp', 'seq')
- frames_grad: float32 [4, 1024, 1024], P('fsdp', 'seq')
- up_first_grad: float32 [1024, 4096], P(('seq', 'fsdp'))
- down_first_grad: float32 [4096, 1024], P(('seq', 'fsdp'))
- joint_qkv_grad: float32 [1024, 3072], P(('seq', 'fsdp'))
- attn_out_grad: float32 [1024, 1024], P(('seq', 'fsdp'))
- conv_in_grad: float32 [1024, 2048], P(('seq', 'fsdp'))
- conv_kernel_grad: float32 [5, 1024], P(None, ('seq', 'fsdp'))
- batch_gain_grad: float32 [1024], P(('seq', 'fsdp'))
- conv_out_grad: float32 [1024, 1024], P(('seq', 'fsdp'))
- up_second_grad: float32 [1024, 4096], P(('seq', 'fsdp'))
- down_second_grad: float32 [4096, 1024], P(('seq', 'fsdp'))
- norm_gains_grad: float32 [5, 1024], P(None, ('seq', 'fsdp'))
- slopes_grad: float32 [8], replicated
Inputs may be any that keep to these rules, and one draw needn't show every extreme that they name: `lengths`: in each bucket one utterance, at a place drawn from the seed, has exactly 897 frames; each other one has at most 32 frames; the frames past the last utterance are padding.
All inputs are finite; a program needn't handle non-finite values.
Results may differ from a plain program's by a relative error of at most 0.025.
Values may be sent and summed in bfloat16 or wider, within the bound.
A program may use at most 448 MiB of HBM per device.

v0:
```python
import math

import jax
import jax.numpy as jnp
from jax import lax
from jax.sharding import PartitionSpec as P

EPSILON = 1e-05
MASKED = -1e30


def extended(x, sides, width):
    for axis, dim in sides:
        size, length = (lax.axis_size(axis), x.shape[dim])
        up = [(i, (i + 1) % size) for i in range(size - 1)]
        down = [(j, i) for i, j in up]
        last = lax.slice_in_dim(x, length - width, length, axis=dim)
        initial = lax.slice_in_dim(x, 0, width, axis=dim)
        before = lax.ppermute(last, axis, up)
        after = lax.ppermute(initial, axis, down)
        x = jnp.concatenate([before, x, after], axis=dim)
    return x


def normed(value, gain):
    average = jnp.mean(value, axis=-1, keepdims=True)
    centred = value - average
    variance = jnp.mean(centred * centred, axis=-1, keepdims=True)
    return centred * lax.rsqrt(variance + EPSILON) * gain


def norm_back(value, gain, gradient):
    pullback = jax.vjp(normed, value, gain)[1]
    return pullback(gradient)


def matmul(left, right):
    return jnp.dot(left, right, preferred_element_type=jnp.float32)


def transposed_left(left, right):
    return lax.dot_general(
        left, right, (((0,), (0,)), ((), ())), preferred_element_type=jnp.float32
    )


def transposed_right(left, right):
    return lax.dot_general(
        left, right, (((1,), (1,)), ((), ())), preferred_element_type=jnp.float32
    )


def item_index(positions, bounds):
    return jnp.sum((positions[:, None] >= bounds[None, :]).astype(jnp.int32), axis=1)


def unpack(weights):
    (
        first_up,
        first_down,
        qkv_full,
        out_full,
        conv_up,
        kernel_full,
        batch_full,
        conv_down,
        second_up,
        second_down,
        gains_full,
    ) = weights
    return (
        first_up,
        first_down,
        qkv_full,
        out_full,
        conv_up,
        kernel_full.astype(jnp.float32),
        batch_full.astype(jnp.float32),
        conv_down,
        second_up,
        second_down,
        gains_full.astype(jnp.float32),
    )


def feed_forward(value, gain, weight_up, weight_down):
    hidden = normed(value, gain).astype(jnp.bfloat16)
    swish = jax.nn.silu(matmul(hidden, weight_up)).astype(jnp.bfloat16)
    return value + 0.5 * matmul(swish, weight_down)


def feed_back(value, gain, weight_up, weight_down, gradient):
    hidden = normed(value, gain).astype(jnp.bfloat16)
    swish, pullback = jax.vjp(jax.nn.silu, matmul(hidden, weight_up))
    swish_low = swish.astype(jnp.bfloat16)
    branch_grad = (0.5 * gradient).astype(jnp.bfloat16)
    down_grad = transposed_left(swish_low, branch_grad)
    active_grad = pullback(transposed_right(branch_grad, weight_down))[0].astype(jnp.bfloat16)
    up_grad = transposed_left(hidden, active_grad)
    value_grad, gain_grad = norm_back(value, gain, transposed_right(active_grad, weight_up))
    return (gradient + value_grad, gain_grad, up_grad, down_grad)


def biased_scores(query_heads, key_heads, slopes, layout):
    query_pos, key_pos, query_ids, key_ids = layout
    raw_scores = jnp.einsum(
        "qhd,khd->hqk", query_heads, key_heads, preferred_element_type=jnp.float32
    )
    distance = jnp.abs(query_pos[:, None] - key_pos[None, :]).astype(jnp.float32)
    scores = (
        raw_scores * (1.0 / math.sqrt(query_heads.shape[2]))
        - slopes[:, None, None] * distance[None]
    )
    shared = query_ids[:, None] == key_ids[None, :]
    return (jnp.where(shared[None], scores, MASKED), distance)


def attention_probs(query, keys, slopes, layout):
    heads = slopes.shape[0]
    head_size = query.shape[1] // heads
    query_heads = query.reshape(query.shape[0], heads, head_size)
    key_heads = keys.reshape(keys.shape[0], heads, head_size)
    scores, distance = biased_scores(query_heads, key_heads, slopes, layout)
    top = jnp.max(scores, axis=-1, keepdims=True)
    exponent = jnp.exp(scores - top)
    total = jnp.sum(exponent, axis=-1, keepdims=True)
    probs = exponent / total
    return (probs, distance, query_heads, key_heads, top[:, :, 0], total[:, :, 0])


def attend(value, gain, weight_qkv, weight_out, slopes, layout):
    feature_width = value.shape[1]
    hidden = normed(value, gain).astype(jnp.bfloat16)
    joint = matmul(hidden, weight_qkv).astype(jnp.bfloat16)
    keys_values = lax.all_gather(joint[:, feature_width:], "seq", axis=0, tiled=True)
    probs, distance, query_heads, key_heads, top, total = attention_probs(
        joint[:, :feature_width], keys_values[:, :feature_width], slopes, layout
    )
    value_heads = keys_values[:, feature_width:].reshape(key_heads.shape)
    mixed = jnp.einsum(
        "hqk,khd->qhd", probs.astype(jnp.bfloat16), value_heads, preferred_element_type=jnp.float32
    )
    mixed = mixed.reshape(value.shape).astype(jnp.bfloat16)
    return (value + matmul(mixed, weight_out), keys_values)


def attend_back(value, gain, weight_qkv, weight_out, slopes, layout, keys_values, gradient):
    feature_width = value.shape[1]
    row_count = value.shape[0]
    hidden = normed(value, gain).astype(jnp.bfloat16)
    joint = matmul(hidden, weight_qkv).astype(jnp.bfloat16)
    probs, distance, query_heads, key_heads, top, total = attention_probs(
        joint[:, :feature_width], keys_values[:, :feature_width], slopes, layout
    )
    probs_low = probs.astype(jnp.bfloat16)
    value_heads = keys_values[:, feature_width:].reshape(key_heads.shape)
    mixed = jnp.einsum("hqk,khd->qhd", probs_low, value_heads, preferred_element_type=jnp.float32)
    mixed = mixed.reshape(value.shape).astype(jnp.bfloat16)
    branch_grad = gradient.astype(jnp.bfloat16)
    weight_out_grad = transposed_left(mixed, branch_grad)
    mixed_flat = transposed_right(branch_grad, weight_out).astype(jnp.bfloat16)
    mixed_grad = mixed_flat.reshape(query_heads.shape)
    prob_grad = jnp.einsum(
        "qhd,khd->hqk", mixed_grad, value_heads, preferred_element_type=jnp.float32
    )
    delta = jnp.sum(probs * prob_grad, axis=-1)
    score_grad = probs * (prob_grad - delta[:, :, None])
    slope_grad = -jnp.sum(score_grad * distance[None], axis=(1, 2))
    scale = 1.0 / math.sqrt(query_heads.shape[2])
    raw_grad = (score_grad * scale).astype(jnp.bfloat16)
    query_grad = jnp.einsum("hqk,khd->qhd", raw_grad, key_heads, preferred_element_type=jnp.float32)
    query_pos, key_pos, query_ids, key_ids = layout
    all_query, all_mixed = (
        lax.all_gather(joint[:, :feature_width], "seq", axis=0, tiled=True),
        lax.all_gather(mixed_flat, "seq", axis=0, tiled=True),
    )
    all_top, all_total, all_delta = (
        lax.all_gather(top, "seq", axis=1, tiled=True),
        lax.all_gather(total, "seq", axis=1, tiled=True),
        lax.all_gather(delta, "seq", axis=1, tiled=True),
    )
    heads = slopes.shape[0]
    head_size = query_heads.shape[2]
    all_query_heads = all_query.reshape(all_query.shape[0], heads, head_size)
    all_mixed_heads = all_mixed.reshape(all_query.shape[0], heads, head_size)
    own_keys = joint[:, feature_width : 2 * feature_width].reshape(row_count, heads, head_size)
    own_values = joint[:, 2 * feature_width :].reshape(row_count, heads, head_size)
    column_scores, column_distance = biased_scores(
        all_query_heads, own_keys, slopes, (key_pos, query_pos, key_ids, query_ids)
    )
    column_probs = jnp.exp(column_scores - all_top[:, :, None]) / all_total[:, :, None]
    column_prob_grad = jnp.einsum(
        "qhd,khd->hqk", all_mixed_heads, own_values, preferred_element_type=jnp.float32
    )
    column_score_grad = column_probs * (column_prob_grad - all_delta[:, :, None])
    column_raw = (column_score_grad * scale).astype(jnp.bfloat16)
    key_grad = jnp.einsum(
        "hqk,qhd->khd", column_raw, all_query_heads, preferred_element_type=jnp.float32
    )
    value_grad = jnp.einsum(
        "hqk,qhd->khd",
        column_probs.astype(jnp.bfloat16),
        all_mixed_heads,
        preferred_element_type=jnp.float32,
    )
    local_grad = jnp.concatenate(
        [key_grad.reshape(row_count, feature_width), value_grad.reshape(row_count, feature_width)],
        axis=1,
    )
    joint_grad = jnp.concatenate([query_grad.reshape(value.shape), local_grad], axis=1).astype(
        jnp.bfloat16
    )
    qkv_grad = transposed_left(hidden, joint_grad)
    input_grad, gain_grad = norm_back(value, gain, transposed_right(joint_grad, weight_qkv))
    return (gradient + input_grad, gain_grad, qkv_grad, weight_out_grad, slope_grad)


def gate_linear(joint):
    feature_width = joint.shape[1] // 2
    return joint[:, :feature_width] * jax.nn.sigmoid(joint[:, feature_width:])


def depthwise(rim, kernel, rim_ids, own_ids):
    row_count = own_ids.shape[0]
    total = jnp.zeros((row_count, rim.shape[1]), jnp.float32)
    for offset in range(kernel.shape[0]):
        shared = (rim_ids[offset : offset + row_count] == own_ids).astype(jnp.float32)
        total = (
            total
            + kernel[offset]
            * rim[offset : offset + row_count].astype(jnp.float32)
            * shared[:, None]
        )
    return total


def depthwise_back(rim, kernel, rim_ids, own_ids, conv_grad):
    row_count = own_ids.shape[0]
    reach = kernel.shape[0] - 1
    grad_rim = extended(conv_grad.astype(jnp.bfloat16), (("seq", 0),), reach // 2).astype(
        conv_grad.dtype
    )
    input_grad = jnp.zeros(conv_grad.shape, jnp.float32)
    kernel_rows = []
    for offset in range(kernel.shape[0]):
        shared = (rim_ids[offset : offset + row_count] == own_ids).astype(jnp.float32)[:, None]
        kernel_rows.append(
            jnp.sum(
                rim[offset : offset + row_count].astype(jnp.float32) * shared * conv_grad, axis=0
            )
        )
        mirror = reach - offset
        crossed = (rim_ids[mirror : mirror + row_count] == own_ids).astype(jnp.float32)[:, None]
        input_grad = input_grad + kernel[offset] * grad_rim[mirror : mirror + row_count] * crossed
    return (input_grad, jnp.stack(kernel_rows))


def body(
    frames,
    lengths,
    up_first,
    down_first,
    joint_qkv,
    attn_out,
    conv_in,
    conv_kernel,
    batch_gain,
    conv_out,
    up_second,
    down_second,
    norm_gains,
    slopes,
    out_grad,
):
    sharded = (
        up_first,
        down_first,
        joint_qkv,
        attn_out,
        conv_in,
        conv_kernel,
        batch_gain,
        conv_out,
        up_second,
        down_second,
        norm_gains,
    )
    gathered = (
        lax.all_gather(sharded[0], "fsdp", axis=0, tiled=True),
        lax.all_gather(sharded[1], "fsdp", axis=0, tiled=True),
        lax.all_gather(sharded[2], "fsdp", axis=0, tiled=True),
        lax.all_gather(sharded[3], "fsdp", axis=0, tiled=True),
        lax.all_gather(sharded[4], "fsdp", axis=0, tiled=True),
        lax.all_gather(sharded[5], "fsdp", axis=1, tiled=True),
        lax.all_gather(sharded[6], "fsdp", axis=0, tiled=True),
        lax.all_gather(sharded[7], "fsdp", axis=0, tiled=True),
        lax.all_gather(sharded[8], "fsdp", axis=0, tiled=True),
        lax.all_gather(sharded[9], "fsdp", axis=0, tiled=True),
        lax.all_gather(sharded[10], "fsdp", axis=1, tiled=True),
    )
    (
        first_up,
        first_down,
        qkv_full,
        out_full,
        conv_up,
        kernel,
        batch_scale,
        conv_down,
        second_up,
        second_down,
        gains,
    ) = unpack(gathered)
    row_count = frames.shape[1]
    feature_width = frames.shape[2]
    seq_count = lax.axis_size("seq")
    start_row = lax.axis_index("seq") * row_count
    bounds = jnp.cumsum(lengths[0])
    item_count = lengths.shape[1]
    own_pos = start_row + jnp.arange(row_count, dtype=jnp.int32)
    key_pos = jnp.arange(row_count * seq_count, dtype=jnp.int32)
    own_ids = item_index(own_pos, bounds)
    layout = (own_pos, key_pos, own_ids, item_index(key_pos, bounds))
    rim_width = conv_kernel.shape[0] // 2
    rim_ids = item_index(
        start_row - rim_width + jnp.arange(row_count + 2 * rim_width, dtype=jnp.int32), bounds
    )
    valid = (own_ids < item_count).astype(jnp.float32)[:, None]
    source = frames[0].astype(jnp.float32)
    first = feed_forward(source, gains[0], first_up, first_down)
    second, keys_values = attend(first, gains[1], qkv_full, out_full, slopes, layout)
    conv_hidden = normed(second, gains[2]).astype(jnp.bfloat16)
    conv_joint = matmul(conv_hidden, conv_up)
    rim = extended(gate_linear(conv_joint).astype(jnp.bfloat16), (("seq", 0),), rim_width)
    conv = depthwise(rim, kernel, rim_ids, own_ids)
    total, count = lax.psum((jnp.sum(valid * conv, axis=0), jnp.sum(valid)), ("seq", "fsdp"))
    average = total / count
    centred = conv - average
    spread = lax.psum(jnp.sum(valid * centred * centred, axis=0), ("seq", "fsdp"))
    variance = spread / count
    inverse = lax.rsqrt(variance + EPSILON)
    standard = (conv - average) * inverse
    pre_swish = standard * batch_scale
    swish, swish_pull = jax.vjp(jax.nn.silu, pre_swish)
    swish_low = swish.astype(jnp.bfloat16)
    third = second + matmul(swish_low, conv_down)
    fourth = feed_forward(third, gains[3], second_up, second_down)
    result = normed(fourth, gains[4])
    regathered = (
        lax.all_gather(sharded[0], "fsdp", axis=0, tiled=True),
        lax.all_gather(sharded[1], "fsdp", axis=0, tiled=True),
        lax.all_gather(sharded[2], "fsdp", axis=0, tiled=True),
        lax.all_gather(sharded[3], "fsdp", axis=0, tiled=True),
        lax.all_gather(sharded[4], "fsdp", axis=0, tiled=True),
        lax.all_gather(sharded[5], "fsdp", axis=1, tiled=True),
        lax.all_gather(sharded[6], "fsdp", axis=0, tiled=True),
        lax.all_gather(sharded[7], "fsdp", axis=0, tiled=True),
        lax.all_gather(sharded[8], "fsdp", axis=0, tiled=True),
        lax.all_gather(sharded[9], "fsdp", axis=0, tiled=True),
        lax.all_gather(sharded[10], "fsdp", axis=1, tiled=True),
    )
    (
        first_up,
        first_down,
        qkv_full,
        out_full,
        conv_up,
        kernel,
        batch_scale,
        conv_down,
        second_up,
        second_down,
        gains,
    ) = unpack(regathered)
    fourth_grad, last_gain = norm_back(fourth, gains[4], out_grad[0].astype(jnp.float32))
    third_grad, fourth_gain, second_up_grad, second_down_grad = feed_back(
        third, gains[3], second_up, second_down, fourth_grad
    )
    branch_grad = third_grad.astype(jnp.bfloat16)
    conv_down_grad = transposed_left(swish_low, branch_grad)
    scaled_grad = swish_pull(transposed_right(branch_grad, conv_down))[0]
    sum_grad, sum_cross = lax.psum(
        (jnp.sum(scaled_grad, axis=0), jnp.sum(scaled_grad * standard, axis=0)), ("seq", "fsdp")
    )
    conv_grad = inverse * (scaled_grad * batch_scale) - valid * (inverse / count) * (
        batch_scale * sum_grad + standard * (batch_scale * sum_cross)
    )
    gated_grad, kernel_grad = depthwise_back(rim, kernel, rim_ids, own_ids, conv_grad)
    joint_pull = jax.vjp(gate_linear, conv_joint)[1]
    joint_grad = joint_pull(gated_grad)[0].astype(jnp.bfloat16)
    conv_up_grad = transposed_left(conv_hidden, joint_grad)
    hidden_grad, third_gain = norm_back(second, gains[2], transposed_right(joint_grad, conv_up))
    second_grad = third_grad + hidden_grad
    late = (
        lax.psum_scatter(second_up_grad, ("seq", "fsdp"), scatter_dimension=0, tiled=True),
        lax.psum_scatter(second_down_grad, ("seq", "fsdp"), scatter_dimension=0, tiled=True),
        lax.psum_scatter(conv_down_grad, ("seq", "fsdp"), scatter_dimension=0, tiled=True),
        lax.psum_scatter(conv_up_grad, ("seq", "fsdp"), scatter_dimension=0, tiled=True),
        lax.psum_scatter(kernel_grad, ("seq", "fsdp"), scatter_dimension=1, tiled=True),
    )
    first_grad, second_gain, qkv_grad, out_weight_grad, slope_part = attend_back(
        first, gains[1], qkv_full, out_full, slopes, layout, keys_values, second_grad
    )
    source_grad, first_gain, first_up_grad, first_down_grad = feed_back(
        source, gains[0], first_up, first_down, first_grad
    )
    gain_grads = jnp.stack([first_gain, second_gain, third_gain, fourth_gain, last_gain])
    early = (
        lax.psum_scatter(first_up_grad, ("seq", "fsdp"), scatter_dimension=0, tiled=True),
        lax.psum_scatter(first_down_grad, ("seq", "fsdp"), scatter_dimension=0, tiled=True),
        lax.psum_scatter(qkv_grad, ("seq", "fsdp"), scatter_dimension=0, tiled=True),
        lax.psum_scatter(out_weight_grad, ("seq", "fsdp"), scatter_dimension=0, tiled=True),
        lax.psum_scatter(gain_grads, ("seq", "fsdp"), scatter_dimension=1, tiled=True),
    )
    slope_grad = lax.psum(slope_part, ("seq", "fsdp"))
    piece_width = feature_width // lax.axis_size(("seq", "fsdp"))
    batch_piece = lax.dynamic_slice_in_dim(
        sum_cross, lax.axis_index(("seq", "fsdp")) * piece_width, piece_width
    )
    return (
        result[None].astype(jnp.bfloat16),
        source_grad[None],
        early[0],
        early[1],
        early[2],
        early[3],
        late[3],
        late[4],
        batch_piece,
        late[2],
        late[0],
        late[1],
        early[4],
        slope_grad,
    )


def solution(mesh):
    placed = (
        P("fsdp", "seq", None),
        P("fsdp", None),
        P("fsdp", None),
        P("fsdp", None),
        P("fsdp", None),
        P("fsdp", None),
        P("fsdp", None),
        P(None, "fsdp"),
        P("fsdp"),
        P("fsdp", None),
        P("fsdp", None),
        P("fsdp", None),
        P(None, "fsdp"),
        P(),
        P("fsdp", "seq", None),
    )
    return jax.shard_map(
        body,
        mesh=mesh,
        in_specs=placed,
        out_specs=(
            P("fsdp", "seq", None),
            P("fsdp", "seq", None),
            P(("seq", "fsdp"), None),
            P(("seq", "fsdp"), None),
            P(("seq", "fsdp"), None),
            P(("seq", "fsdp"), None),
            P(("seq", "fsdp"), None),
            P(None, ("seq", "fsdp")),
            P(("seq", "fsdp")),
            P(("seq", "fsdp"), None),
            P(("seq", "fsdp"), None),
            P(("seq", "fsdp"), None),
            P(None, ("seq", "fsdp")),
            P(),
        ),
        check_vma=False,
    )
```

profile of v0, /device:TPU:4, one launch (start us, length us, event | category | flops | bytes accessed | tf_op | source)
XLA Modules:
  0.0 3425.1 jit_solution(11297560276942240660)
XLA Ops:
  9.5 13.4 all_gather.62
  24.3 136.2 %all-gather.13.cloned.1.call-done = bf16[1024,4096]{1,0:T(8,128)(2,1)} async-done(((bf16[256,4096]{1,0:T(8,128)(2,1)}), bf16[1024,4096]{1,0:T(8,128)(2,1)}) %all-gather.13.cloned.1.call-update) | async-done | bytes 8388624 | tf_op jit(solution)/shard_map/all_gather | solution.py:289
  160.5 4.7 fusion.130
  165.2 144.7 %all-gather.15.cloned.1.call-done = bf16[4096,1024]{1,0:T(8,128)(2,1)} async-done(((bf16[1024,1024]{1,0:T(8,128)(2,1)}), bf16[4096,1024]{1,0:T(8,128)(2,1)}) %all-gather.15.cloned.1.call-update) | async-done | bytes 8388624 | tf_op jit(solution)/shard_map/all_gather | solution.py:290
  309.9 4.8 fusion.152
  315.0 110.2 %all-gather.17.cloned.1.call-done = bf16[1024,3072]{1,0:T(8,128)(2,1)} async-done(((bf16[256,3072]{1,0:T(8,128)(2,1)}), bf16[1024,3072]{1,0:T(8,128)(2,1)}) %all-gather.17.cloned.1.call-update) | async-done | bytes 6291472 | tf_op jit(solution)/shard_map/all_gather | solution.py:291
  425.1 3.8 convolution_convert_fusion
  433.5 13.4 all_gather.68
  449.9 14.9 all-gather.19.cloned.1.call-done
  464.8 4.2 fusion.146
  469.1 2.6 copy.65
  471.6 3.1 fusion.2
  477.9 2.8 fusion.27
  480.7 31.6 all-gather.21.cloned.1.call-done
  512.3 2.2 fusion.153
  515.0 78.4 %all-gather.23.cloned.1.call-done = bf16[1024,2048]{1,0:T(8,128)(2,1)} async-done(((bf16[256,2048]{1,0:T(8,128)(2,1)}), bf16[1024,2048]{1,0:T(8,128)(2,1)}) %all-gather.23.cloned.1.call-update) | async-done | bytes 4194320 | tf_op jit(solution)/shard_map/all_gather | solution.py:293
  593.3 3.0 fusion.133
  596.5 2.8 collective-permute-start.1
  601.8 8.8 all-gather
  611.4 42.1 %all-reduce.3 = (f32[1024]{0:T(1024)S(1)}, f32[]{:T(128)}) all-reduce(f32[1024]{0:T(1024)S(1)} %get-tuple-element.48, f32[]{:T(128)} %fusion.125), channel_id=1, replica_groups=mesh['seq'=8,'fsdp'=4] {'seq','fsdp'}, use_global_device_ids=true, to_apply=%region_13.14 | all-reduce | flops 1025 | bytes 8200 | tf_op jit(solution)/shard_map/psum | solution.py:336
  654.4 46.3 %psum.44 = f32[1024]{0:T(1024)S(1)} all-reduce(f32[1024]{0:T(1024)S(1)} %fusion.67), channel_id=1, replica_groups=mesh['seq'=8,'fsdp'=4] {'seq','fsdp'}, use_global_device_ids=true, to_apply=%region_17.18 | all-reduce | flops 1024 | bytes 8192 | tf_op jit(solution)/shard_map/psum | solution.py:339
  704.3 87.1 %all-gather.27.cloned.1.call-done = bf16[1024,4096]{1,0:T(8,128)(2,1)} async-done(((bf16[256,4096]{1,0:T(8,128)(2,1)}), bf16[1024,4096]{1,0:T(8,128)(2,1)}) %all-gather.27.cloned.1.call-update) | async-done | bytes 8388624 | tf_op jit(solution)/shard_map/all_gather | solution.py:297
  791.5 6.1 fusion.135
  797.6 143.3 %all-gather.29.cloned.1.call-done = bf16[4096,1024]{1,0:T(8,128)(2,1)} async-done(((bf16[1024,1024]{1,0:T(8,128)(2,1)}), bf16[4096,1024]{1,0:T(8,128)(2,1)}) %all-gather.29.cloned.1.call-update) | async-done | bytes 8388624 | tf_op jit(solution)/shard_map/all_gather | solution.py:298
  941.0 5.6 fusion.155
  948.6 3.2 fusion.5
  951.9 3.5 multiply_reduce_fusion.2
  955.9 2.3 fusion.139
  958.2 40.1 %all-reduce.2 = (f32[1024]{0:T(1024)}, f32[1024]{0:T(1024)}) all-reduce(f32[1024]{0:T(1024)} %get-tuple-element.32, f32[1024]{0:T(1024)} %get-tuple-element.31), channel_id=1, replica_groups=mesh['seq'=8,'fsdp'=4] {'seq','fsdp'}, use_global_device_ids=true, to_apply=%region_29.30 | all-reduce | flops 2048 | bytes 16384 | tf_op jit(solution)/shard_map/psum | solution.py:382
  999.0 3.5 fusion.65
  1004.5 2.4 collective-permute-start.2
  1006.9 3.4 collective-permute-done.2
  1020.0 2.9 copy.66
  1022.9 7.3 all_gather.76
  1030.2 9.8 all_gather.75
  1040.1 5.8 exponential_divide_fusion
  1047.8 5.4 multiply_reduce_fusion.1
  1053.2 9.3 all_gather.78
  1062.5 3.0 fusion.32
  1065.6 3.1 copy.67
  1068.6 3.6 fusion.24
  1072.3 5.6 fusion.23
  1077.9 6.1 multiply_reduce_fusion.4
  1085.2 6.6 fusion.8
  1091.9 3.0 fusion.46
  1099.9 3.4 fusion.102
  1103.4 3.7 fusion.99
  1107.8 4.6 fusion.110
  1113.5 6.5 fusion.83
  1121.3 8.2 fusion.134
  1131.2 8.2 fusion.126
  1140.6 8.2 fusion.128
  1150.6 8.1 fusion.108
  1159.8 4.9 multiply_reduce_fusion
  1166.0 41.9 %psum.47 = f32[8]{0:T(128)} all-reduce(f32[8]{0:T(128)S(1)} %neg.45), channel_id=1, replica_groups=mesh['seq'=8,'fsdp'=4] {'seq','fsdp'}, use_global_device_ids=true, to_apply=%region_58.59 | all-reduce | flops 8 | bytes 64 | tf_op jit(solution)/shard_map/psum | solution.py:415
  1210.3 102.7 %reduce-scatter.33.cloned.1.call-done = f32[32,5]{1,0:T(8,128)} async-done(((f32[1024,5]{1,0:T(8,128)}), f32[32,5]{1,0:T(8,128)}) %reduce-scatter.33.cloned.1.call-update) | async-done | bytes 656
  1314.4 146.0 %reduce-scatter.25.cloned.1.call-done = f32[32,1024]{1,0:T(8,128)} async-done(((f32[1024,1024]{1,0:T(8,128)}), f32[32,1024]{1,0:T(8,128)}) %reduce-scatter.25.cloned.1.call-update) | async-done | bytes 131088 | tf_op jit(solution)/shard_map/reduce_scatter | solution.py:397
  1460.4 149.8 %reduce-scatter.21.cloned.1.call-done = f32[32,1024]{1,0:T(8,128)} async-done(((f32[1024,1024]{1,0:T(8,128)}), f32[32,1024]{1,0:T(8,128)}) %reduce-scatter.21.cloned.1.call-update) | async-done | bytes 131088 | tf_op jit(solution)/shard_map/reduce_scatter | solution.py:412
  1610.2 186.5 %reduce-scatter.23.cloned.1.call-done = f32[32,2048]{1,0:T(8,128)} async-done(((f32[1024,2048]{1,0:T(8,128)}), f32[32,2048]{1,0:T(8,128)}) %reduce-scatter.23.cloned.1.call-update) | async-done | bytes 262160 | tf_op jit(solution)/shard_map/reduce_scatter | solution.py:398
  1796.7 160.7 %reduce-scatter.19.cloned.1.call-done = f32[32,3072]{1,0:T(8,128)} async-done(((f32[1024,3072]{1,0:T(8,128)}), f32[32,3072]{1,0:T(8,128)}) %reduce-scatter.19.cloned.1.call-update) | async-done | bytes 393232 | tf_op jit(solution)/shard_map/reduce_scatter | solution.py:411
  1957.4 365.3 %reduce-scatter.27.cloned.1.call-done = f32[32,4096]{1,0:T(8,128)} async-done(((f32[1024,4096]{1,0:T(8,128)}), f32[32,4096]{1,0:T(8,128)}) %reduce-scatter.27.cloned.1.call-update) | async-done | bytes 524304 | tf_op jit(solution)/shard_map/reduce_scatter | solution.py:395
  2322.7 365.1 %reduce-scatter.29.cloned.1.call-done = f32[128,1024]{1,0:T(8,128)} async-done(((f32[4096,1024]{1,0:T(8,128)}), f32[128,1024]{1,0:T(8,128)}) %reduce-scatter.29.cloned.1.call-update) | async-done | bytes 524304 | tf_op jit(solution)/shard_map/reduce_scatter | solution.py:396
  2687.8 365.0 %reduce-scatter.15.cloned.1.call-done = f32[32,4096]{1,0:T(8,128)} async-done(((f32[1024,4096]{1,0:T(8,128)}), f32[32,4096]{1,0:T(8,128)}) %reduce-scatter.15.cloned.1.call-update) | async-done | bytes 524304 | tf_op jit(solution)/shard_map/reduce_scatter | solution.py:409
  3052.8 365.2 %reduce-scatter.17.cloned.1.call-done = f32[128,1024]{1,0:T(8,128)} async-done(((f32[4096,1024]{1,0:T(8,128)}), f32[128,1024]{1,0:T(8,128)}) %reduce-scatter.17.cloned.1.call-update) | async-done | bytes 524304 | tf_op jit(solution)/shard_map/reduce_scatter | solution.py:410
  (384 shorter events, 58.7 us)
Async XLA Ops:
  7.2 153.3 %all-gather.13.cloned.1.call-start = ((), (), s32[]{:S(2)}) async-start(), calls=%async_computation.10 | async-start | bytes 10485760 | tf_op jit(solution)/shard_map/all_gather | solution.py:289
  7.9 302.0 %all-gather.15.cloned.1.call-start = ((), (), s32[]{:S(2)}) async-start(), calls=%async_computation.11 | async-start | bytes 10485760 | tf_op jit(solution)/shard_map/all_gather | solution.py:290
  8.7 416.4 %all-gather.17.cloned.1.call-start = ((), (), s32[]{:S(2)}) async-start(), calls=%async_computation.12 | async-start | bytes 7864320 | tf_op jit(solution)/shard_map/all_gather | solution.py:291
  9.4 455.4 %all-gather.19.cloned.1.call-start = ((), (), s32[]{:S(2)}) async-start(), calls=%async_computation.13 | async-start | bytes 4718592 | tf_op jit(solution)/shard_map/all_gather | solution.py:135
  23.0 142.2 %copy-start.64 = (f32[128]{0:T(128)}, f32[128]{0:T(128)S(1)}, u32[]{:S(2)}) copy-start(f32[128]{0:T(128)S(1)} %broadcast_multiply_fusion.4) | copy-start | bytes 1540
  23.7 141.5 %copy-start.70 = (f32[128]{0:T(128)}, f32[128]{0:T(128)S(1)}, u32[]{:S(2)}) copy-start(f32[128]{0:T(128)S(1)} %fusion.112) | copy-start | bytes 1540
  165.2 149.5 %copy-start.6 = (f32[128,4096]{1,0:T(8,128)}, f32[128,4096]{1,0:T(8,128)S(1)}, u32[]{:S(2)}) copy-start(f32[128,4096]{1,0:T(8,128)S(1)} %fusion.130) | copy-start | bytes 6291460
  314.7 197.6 %copy-start.4 = (f32[128,1024]{1,0:T(8,128)}, f32[128,1024]{1,0:T(8,128)S(1)}, u32[]{:S(2)}) copy-start(f32[128,1024]{1,0:T(8,128)S(1)} %get-tuple-element.82) | copy-start | bytes 1572868
  314.7 115.1 %copy-start.86 = (f32[128]{0:T(128)}, f32[128]{0:T(128)S(1)}, u32[]{:S(2)}) copy-start(f32[128]{0:T(128)S(1)} %broadcast_multiply_fusion.3) | copy-start | bytes 1540
  314.9 114.9 %copy-start.113 = (f32[128]{0:T(128)}, f32[128]{0:T(128)S(1)}, u32[]{:S(2)}) copy-start(f32[128]{0:T(128)S(1)} %multiply_reduce_fusion.13) | copy-start | bytes 1540
  315.0 114.9 %copy-start.89 = (f32[128]{0:T(128)}, f32[128]{0:T(128)S(1)}, u32[]{:S(2)}) copy-start(f32[128]{0:T(128)S(1)} %fusion.113) | copy-start | bytes 1540
  429.9 82.5 %all-gather.21.cloned.1.call-start = ((), (), s32[]{:S(2)}) async-start(), calls=%async_computation.14 | async-start | bytes 2621440 | tf_op jit(solution)/shard_map/all_gather | solution.py:292
  430.5 162.9 %all-gather.23.cloned.1.call-start = ((), (), s32[]{:S(2)}) async-start(), calls=%async_computation.15 | async-start | bytes 5242880 | tf_op jit(solution)/shard_map/all_gather | solution.py:293
  431.0 270.9 %all-gather.25.cloned.1.call-start = ((), (), s32[]{:S(2)}) async-start(), calls=%async_computation.16 | async-start | bytes 2621440 | tf_op jit(solution)/shard_map/all_gather | solution.py:296
  431.8 359.7 %all-gather.27.cloned.1.call-start = ((), (), s32[]{:S(2)}) async-start(), calls=%async_computation.17 | async-start | bytes 10485760 | tf_op jit(solution)/shard_map/all_gather | solution.py:297
  432.5 508.4 %all-gather.29.cloned.1.call-start = ((), (), s32[]{:S(2)}) async-start(), calls=%async_computation.18 | async-start | bytes 10485760 | tf_op jit(solution)/shard_map/all_gather | solution.py:298
  433.3 586.8 %all-gather.31.cloned.1.call-start = ((), (), s32[]{:S(2)}) async-start(), calls=%async_computation.19 | async-start | bytes 2359296 | tf_op jit(solution)/shard_map/all_gather | solution.py:174
  448.8 27.4 copy-start.17
  514.6 86.6 %copy-start.99 = (s32[128]{0:T(128)S(1)}, s32[128]{0:T(128)}, u32[]{:S(2)}) copy-start(s32[128]{0:T(128)} %copy-done.98) | copy-start | bytes 1540
  514.6 87.2 %copy-start.122 = (bf16[256]{0:T(256)(128)(2,1)S(1)}, bf16[256]{0:T(256)(128)(2,1)}, u32[]{:S(2)}) copy-start(bf16[256]{0:T(256)(128)(2,1)} %param.23) | copy-start | bytes 1540
  514.6 96.2 %copy-start.59 = (f32[1,1024]{1,0:T(1,128)S(1)}, f32[1,1024]{1,0:T(1,128)}, u32[]{:S(2)}) copy-start(f32[1,1024]{1,0:T(1,128)} %get-tuple-element.66) | copy-start | bytes 12292
  514.6 96.2 %copy-start.60 = (f32[1,1024]{1,0:T(1,128)S(1)}, f32[1,1024]{1,0:T(1,128)}, u32[]{:S(2)}) copy-start(f32[1,1024]{1,0:T(1,128)} %get-tuple-element.67) | copy-start | bytes 12292
  514.6 96.2 %copy-start.61 = (f32[1,1024]{1,0:T(1,128)S(1)}, f32[1,1024]{1,0:T(1,128)}, u32[]{:S(2)}) copy-start(f32[1,1024]{1,0:T(1,128)} %get-tuple-element.68) | copy-start | bytes 12292
  514.6 96.2 %copy-start.62 = (f32[1,1024]{1,0:T(1,128)S(1)}, f32[1,1024]{1,0:T(1,128)}, u32[]{:S(2)}) copy-start(f32[1,1024]{1,0:T(1,128)} %get-tuple-element.69) | copy-start | bytes 12292
  514.7 96.2 %copy-start.63 = (f32[1,1024]{1,0:T(1,128)S(1)}, f32[1,1024]{1,0:T(1,128)}, u32[]{:S(2)}) copy-start(f32[1,1024]{1,0:T(1,128)} %get-tuple-element.70) | copy-start | bytes 12292
  514.7 96.2 %copy-start.92 = (f32[128]{0:T(128)S(1)}, f32[128]{0:T(128)}, u32[]{:S(2)}) copy-start(f32[128]{0:T(128)} %get-tuple-element.80) | copy-start | bytes 1540
  514.7 96.2 %copy-start.93 = (f32[128]{0:T(128)S(1)}, f32[128]{0:T(128)}, u32[]{:S(2)}) copy-start(f32[128]{0:T(128)} %get-tuple-element.75) | copy-start | bytes 1540
  514.7 96.2 %copy-start.94 = (f32[128]{0:T(128)S(1)}, f32[128]{0:T(128)}, u32[]{:S(2)}) copy-start(f32[128]{0:T(128)} %get-tuple-element.76) | copy-start | bytes 1540
  514.7 96.2 %copy-start.95 = (f32[128]{0:T(128)S(1)}, f32[128]{0:T(128)}, u32[]{:S(2)}) copy-start(f32[128]{0:T(128)} %get-tuple-element.77) | copy-start | bytes 1540
  514.7 96.2 %copy-start.96 = (f32[128]{0:T(128)S(1)}, f32[128]{0:T(128)}, u32[]{:S(2)}) copy-start(f32[128]{0:T(128)} %get-tuple-element.78) | copy-start | bytes 1540
  514.7 96.2 %copy-start.97 = (f32[128]{0:T(128)S(1)}, f32[128]{0:T(128)}, u32[]{:S(2)}) copy-start(f32[128]{0:T(128)} %get-tuple-element.79) | copy-start | bytes 1540
  514.7 87.1 %copy-start.76 = (f32[128]{0:T(128)}, f32[128]{0:T(128)S(1)}, u32[]{:S(2)}) copy-start(f32[128]{0:T(128)S(1)} %broadcast_multiply_fusion.2) | copy-start | bytes 1540
  514.9 84.3 %copy-start.115 = (f32[128]{0:T(128)}, f32[128]{0:T(128)S(1)}, u32[]{:S(2)}) copy-start(f32[128]{0:T(128)S(1)} %multiply_reduce_fusion.12) | copy-start | bytes 1540
  515.0 81.5 %copy-start.83 = (f32[128]{0:T(128)}, f32[128]{0:T(128)S(1)}, u32[]{:S(2)}) copy-start(f32[128]{0:T(128)S(1)} %fusion.114) | copy-start | bytes 1540
  596.5 201.1 %copy-start.38 = (bf16[128,1024]{1,0:T(8,128)(2,1)}, bf16[128,1024]{1,0:T(8,128)(2,1)S(1)}, u32[]{:S(2)}) copy-start(bf16[128,1024]{1,0:T(8,128)(2,1)S(1)} %multiply_convert_fusion.12) | copy-start | bytes 786436
  596.5 14.3 collective-permute-start.1
  599.3 11.5 collective-permute-start
  610.7 186.9 %copy-start.47 = (f32[4,1,256]{2,1,0:T(1,128)}, f32[4,1,256]{2,1,0:T(1,128)S(1)}, u32[]{:S(2)}) copy-start(f32[4,1,256]{2,1,0:T(1,128)S(1)} %convert_element_type.246) | copy-start | bytes 12292
  610.7 454.9 %all-gather.33.cloned.1.call-start = ((), (), s32[]{:S(2)}) async-start(), calls=%async_computation.20 | async-start | bytes 2359296 | tf_op jit(solution)/shard_map/all_gather | solution.py:175
  610.8 186.8 %copy-start.81 = (bf16[2,1024]{1,0:T(2,128)(2,1)}, bf16[2,1024]{1,0:T(2,128)(2,1)S(1)}, u32[]{:S(2)}) copy-start(bf16[2,1024]{1,0:T(2,128)(2,1)S(1)} %collective-permute-done.1) | copy-start | bytes 12292
  610.8 186.8 %copy-start.82 = (bf16[2,1024]{1,0:T(2,128)(2,1)}, bf16[2,1024]{1,0:T(2,128)(2,1)S(1)}, u32[]{:S(2)}) copy-start(bf16[2,1024]{1,0:T(2,128)(2,1)S(1)} %collective-permute-done) | copy-start | bytes 12292
  611.4 387.6 %copy-start.12 = (f32[128,1024]{1,0:T(8,128)}, f32[128,1024]{1,0:T(8,128)S(1)}, u32[]{:S(2)}) copy-start(f32[128,1024]{1,0:T(8,128)S(1)} %get-tuple-element.49) | copy-start | bytes 1572868
  654.3 143.3 %copy-start.45 = (f32[1024]{0:T(1024)}, f32[1024]{0:T(1024)S(1)}, u32[]{:S(2)}) copy-start(f32[1024]{0:T(1024)S(1)} %broadcast_divide_fusion.1) | copy-start | bytes 12292
  701.9 95.7 %copy-start.57 = (f32[1024]{0:T(1024)}, f32[1024]{0:T(1024)S(1)}, u32[]{:S(2)}) copy-start(f32[1024]{0:T(1024)S(1)} %get-tuple-element.72) | copy-start | bytes 12292
  704.1 93.5 %copy-start.67 = (f32[128]{0:T(128)}, f32[128]{0:T(128)S(1)}, u32[]{:S(2)}) copy-start(f32[128]{0:T(128)S(1)} %broadcast_multiply_fusion.1) | copy-start | bytes 1540
  704.3 93.3 %copy-start.117 = (f32[128]{0:T(128)}, f32[128]{0:T(128)S(1)}, u32[]{:S(2)}) copy-start(f32[128]{0:T(128)S(1)} %multiply_reduce_fusion.10) | copy-start | bytes 1540
  704.3 93.3 %copy-start.73 = (f32[128]{0:T(128)}, f32[128]{0:T(128)S(1)}, u32[]{:S(2)}) copy-start(f32[128]{0:T(128)S(1)} %fusion.115) | copy-start | bytes 1540
  955.9 55.9 %copy-start.20 = (f32[128,1024]{1,0:T(8,128)}, f32[128,1024]{1,0:T(8,128)S(1)}, u32[]{:S(2)}) copy-start(f32[128,1024]{1,0:T(8,128)S(1)} %add_add_fusion.7) | copy-start | bytes 1572868
  1002.6 4.3 collective-permute-start.3
  1004.5 5.8 collective-permute-start.2
  1017.0 190.8 %reduce-scatter.31.cloned.1.call-start = ((), (), s32[]{:S(2)}) async-start(), calls=%async_computation.29 | async-start | bytes 540672
  1022.9 23.0 copy-start.11
  1047.7 265.3 %reduce-scatter.33.cloned.1.call-start = ((), (), s32[]{:S(2)}) async-start(), calls=%async_computation.30 | async-start | bytes 540672
  1099.8 360.6 %reduce-scatter.25.cloned.1.call-start = ((), (), s32[]{:S(2)}) async-start(), calls=%async_computation.26 | async-start | bytes 4325376 | tf_op jit(solution)/shard_map/reduce_scatter | solution.py:397
  1103.3 506.9 %reduce-scatter.21.cloned.1.call-start = ((), (), s32[]{:S(2)}) async-start(), calls=%async_computation.24 | async-start | bytes 4325376 | tf_op jit(solution)/shard_map/reduce_scatter | solution.py:412
  1107.1 689.6 %reduce-scatter.23.cloned.1.call-start = ((), (), s32[]{:S(2)}) async-start(), calls=%async_computation.25 | async-start | bytes 8650752 | tf_op jit(solution)/shard_map/reduce_scatter | solution.py:398
  1112.5 844.9 %reduce-scatter.19.cloned.1.call-start = ((), (), s32[]{:S(2)}) async-start(), calls=%async_computation.23 | async-start | bytes 12976128 | tf_op jit(solution)/shard_map/reduce_scatter | solution.py:411
  1120.1 1202.6 %reduce-scatter.27.cloned.1.call-start = ((), (), s32[]{:S(2)}) async-start(), calls=%async_computation.27 | async-start | bytes 17301504 | tf_op jit(solution)/shard_map/reduce_scatter | solution.py:395
  1129.6 1558.2 %reduce-scatter.29.cloned.1.call-start = ((), (), s32[]{:S(2)}) async-start(), calls=%async_computation.28 | async-start | bytes 17301504 | tf_op jit(solution)/shard_map/reduce_scatter | solution.py:396
  1139.4 1913.4 %reduce-scatter.15.cloned.1.call-start = ((), (), s32[]{:S(2)}) async-start(), calls=%async_computation.21 | async-start | bytes 17301504 | tf_op jit(solution)/shard_map/reduce_scatter | solution.py:409
  1148.9 2269.1 %reduce-scatter.17.cloned.1.call-start = ((), (), s32[]{:S(2)}) async-start(), calls=%async_computation.22 | async-start | bytes 17301504 | tf_op jit(solution)/shard_map/reduce_scatter | solution.py:410
  1159.8 49.4 %copy-start.112 = (f32[128]{0:T(128)S(1)}, f32[128]{0:T(128)}, u32[]{:S(2)}) copy-start(f32[128]{0:T(128)} %get-tuple-element.25) | copy-start | bytes 1540
  1159.8 49.4 %copy-start.26 = (f32[128,1024]{1,0:T(8,128)S(1)}, f32[128,1024]{1,0:T(8,128)}, u32[]{:S(2)}) copy-start(f32[128,1024]{1,0:T(8,128)} %copy-done.25) | copy-start | bytes 1572868
  1159.8 49.4 %copy-start.109 = (f32[128]{0:T(128)S(1)}, f32[128]{0:T(128)}, u32[]{:S(2)}) copy-start(f32[128]{0:T(128)} %copy-done.108) | copy-start | bytes 1540
  (88 other events, 420.1 us)
Sparse Core Ops, SparseCore 0:
  9.6 150.8 all-gather.12
  162.0 147.8 all-gather.14
  311.5 113.5 all-gather.16
  430.0 34.7 all-gather.18
  466.2 46.0 all-gather.20
  513.8 79.5 all-gather.22
  594.9 45.4 all-gather.24
  641.9 149.4 all-gather.26
  793.0 147.8 all-gather.28
  942.7 26.5 all-gather.30
  1017.1 27.0 all-gather.32
  1047.8 132.3 reduce-scatter.30
  1182.5 130.4 reduce-scatter.32
  1315.7 144.6 reduce-scatter.24
  1463.1 147.0 reduce-scatter.20
  1612.9 183.7 reduce-scatter.22
  1803.2 154.1 reduce-scatter.18
  1960.2 362.4 reduce-scatter.26
  2325.7 362.0 reduce-scatter.28
  2690.6 362.1 reduce-scatter.14
  3055.8 362.1 reduce-scatter.16
where the time goes:
time: 3430 us
  waiting for transfers between devices  2960 us (86%)
  blocking collectives  232 us (7%)
  matrix products  141 us (4%)
  local copies, waits for them, and re-layouts  37.4 us (1%)
    reduce_scatter x1, waiting for transfers between devices, body(): lax.psum_scatter(second_up_grad, ('seq', 'fsdp'), scatter_dimension=0, ti...  365 us
    reduce_scatter x1, waiting for transfers between devices, body(): lax.psum_scatter(first_down_grad, ('seq', 'fsdp'), scatter_dimension=0, t...  365 us
    reduce_scatter x1, waiting for transfers between devices, body(): lax.psum_scatter(second_down_grad, ('seq', 'fsdp'), scatter_dimension=0,...  365 us
    reduce_scatter x1, waiting for transfers between devices, body(): lax.psum_scatter(first_up_grad, ('seq', 'fsdp'), scatter_dimension=0, til...  365 us
    reduce_scatter x1, waiting for transfers between devices, body(): lax.psum_scatter(conv_up_grad, ('seq', 'fsdp'), scatter_dimension=0, tile...  187 us
    reduce_scatter x1, waiting for transfers between devices, body(): lax.psum_scatter(qkv_grad, ('seq', 'fsdp'), scatter_dimension=0, tiled=True)  161 us
    reduce_scatter x1, waiting for transfers between devices, body(): lax.psum_scatter(out_weight_grad, ('seq', 'fsdp'), scatter_dimension=0, t...  150 us
    reduce_scatter x1, waiting for transfers between devices, body(): lax.psum_scatter(conv_down_grad, ('seq', 'fsdp'), scatter_dimension=0, ti...  146 us
  transfers between devices with their start and end apart: 25, of which 18 were waited for; matrix products, arithmetic and copies ran while one was open for 5% of the time, Pallas kernels for 0%

commit v1 on v0

--- a/solution.py
+++ b/solution.py
@@ -1,8 +1,11 @@
+import functools
 import math
 
 import jax
 import jax.numpy as jnp
 from jax import lax
+from jax.experimental import pallas as pl
+from jax.experimental.pallas import tpu as pltpu
 from jax.sharding import PartitionSpec as P
 
 EPSILON = 1e-05
@@ -435,7 +438,1115 @@
     )
 
 
+BF = jnp.bfloat16
+F32 = jnp.float32
+MESH = pl.DeviceIdType.MESH
+GRANT = 56 * 2**20
+CHIPS = 4
+SLOTS = 96
+
+
+def mm(left, right):
+    return jnp.dot(left, right, preferred_element_type=F32)
+
+
+def mm_right(left, right):
+    return lax.dot_general(left, right, (((1,), (1,)), ((), ())), preferred_element_type=F32)
+
+
+def mm_left(left, right):
+    return lax.dot_general(left, right, (((0,), (0,)), ((), ())), preferred_element_type=F32)
+
+
+class Here:
+    def __init__(self, planes):
+        self.planes = planes
+        self.seq = lax.axis_index("seq")
+        self.plane = lax.axis_index("fsdp")
+        self.core = lax.rem(self.seq, 2)
+        self.chip = lax.div(self.seq, 2)
+        column, row = lax.rem(self.chip, 2), lax.div(self.chip, 2)
+        self.chips = [
+            lax.rem(row + j // 2, 2) * 2 + lax.rem(column + j % 2, 2) for j in range(CHIPS)
+        ]
+
+    def peer(self, slot):
+        return (self.chips[slot] * 2 + self.core, self.plane)
+
+    def cross(self, slot):
+        return (self.chips[slot] * 2 + 1 - self.core, self.plane)
+
+    def sibling(self):
+        return self.cross(0)
+
+    def level(self, step):
+        return lax.rem(self.plane + step, self.planes)
+
+    def above(self, step):
+        return (self.seq, self.level(step))
+
+    def rows(self, slot, height):
+        return pl.ds(pl.multiple_of((self.chips[slot] * 2 + self.core) * height, height), height)
+
+    def other_rows(self, slot, height):
+        return pl.ds(pl.multiple_of((self.chips[slot] * 2 + 1 - self.core) * height, height), height)
+
+
+class Mail:
+    def __init__(self, send, recv):
+        self.send, self.recv, self.count, self.open = send, recv, 0, []
+
+    def slot(self):
+        self.count += 1
+        return self.count - 1
+
+    def post(self, src, dst, device):
+        i = self.slot()
+        copy = pltpu.make_async_remote_copy(
+            src_ref=src,
+            dst_ref=dst,
+            send_sem=self.send.at[i],
+            recv_sem=self.recv.at[i],
+            device_id=device,
+            device_id_type=MESH,
+        )
+        copy.start()
+        self.open.append(copy)
+        return copy
+
+    def local(self, src, dst):
+        copy = pltpu.make_async_copy(src, dst, self.send.at[self.slot()])
+        copy.start()
+        return copy
+
+    def close(self):
+        for copy in self.open:
+            copy.wait_send()
+        self.open = []
+
+
+def greet(devices):
+    barrier = pltpu.get_barrier_semaphore()
+    for device in devices:
+        pl.semaphore_signal(barrier, inc=1, device_id=device, device_id_type=MESH)
+    pl.semaphore_wait(barrier, len(devices))
+
+
+def greet_near(here):
+    greet(
+        [here.peer(j) for j in range(1, CHIPS)]
+        + [here.sibling()]
+        + [here.above(k) for k in range(1, here.planes)]
+    )
+
+
+def spread(mail, here, buf):
+    return [None] + [mail.post(buf.at[0], buf.at[j], here.peer(j)) for j in range(1, CHIPS)]
+
+
+def arrive(copies, slot):
+    if copies[slot] is not None:
+        copies[slot].wait_recv()
+
+
+def over_planes(mail, here, src, piece):
+    own = mail.local(src, piece(here.plane))
+    others = [mail.post(src, piece(here.plane), here.above(k)) for k in range(1, here.planes)]
+
+    def wait():
+        own.wait()
+        for copy in others:
+            copy.wait_recv()
+
+    return wait
+
+
+def from_plane(mail, here, src, dst, source):
+    arrived = mail.slot()
+    places = [mail.slot() for _ in range(1, here.planes)]
+    own = pltpu.make_async_copy(src, dst, mail.send.at[arrived])
+    copies = [
+        pltpu.make_async_remote_copy(
+            src_ref=src,
+            dst_ref=dst,
+            send_sem=mail.send.at[places[k - 1]],
+            recv_sem=mail.recv.at[arrived],
+            device_id=here.above(k),
+            device_id_type=MESH,
+        )
+        for k in range(1, here.planes)
+    ]
+
+    @pl.when(here.plane == source)
+    def _():
+        own.start()
+        for copy in copies:
+            copy.start()
+
+    def wait():
+        @pl.when(here.plane == source)
+        def _():
+            own.wait()
+            for copy in copies:
+                copy.wait_send()
+
+        @pl.when(here.plane != source)
+        def _():
+            copies[0].wait_recv()
+
+    return wait
+
+
+def sum_over_planes(mail, here, parts, land):
+    copies = [
+        mail.post(parts.at[here.level(k)], land.at[k - 1], here.above(k))
+        for k in range(1, here.planes)
+    ]
+
+    def total():
+        for copy in copies:
+            copy.wait_recv()
+        value = parts[here.plane].astype(F32)
+        for k in range(1, here.planes):
+            value = value + land[k - 1].astype(F32)
+        return value
+
+    return total
+
+
+def scale_row(small_ref, index):
+    rows = [small_ref[k].astype(F32)[index : index + 1, :] for k in range(small_ref.shape[0])]
+    return jnp.concatenate(rows, axis=1)
+
+
+def own_channels(small_ref, here, index, width):
+    block = small_ref[here.chip, :, pl.ds(pl.multiple_of(here.core * width, width), width)]
+    return block.astype(F32)[index, :]
+
+
+def whitened(value):
+    average = jnp.mean(value, axis=-1, keepdims=True)
+    centred = value - average
+    inverse = lax.rsqrt(jnp.mean(centred * centred, axis=-1, keepdims=True) + EPSILON)
+    return centred * inverse, inverse
+
+
+def norm_grad(value, gain, gradient):
+    white, inverse = whitened(value)
+    inner = gradient * gain
+    value_grad = inverse * (
+        inner
+        - jnp.mean(inner, axis=-1, keepdims=True)
+        - white * jnp.mean(inner * white, axis=-1, keepdims=True)
+    )
+    return value_grad, jnp.sum(gradient * white, axis=0, keepdims=True)
+
+
+def at_row(index, row, height=8):
+    place = lax.broadcasted_iota(jnp.int32, (height, row.shape[1]), 0)
+    return jnp.where(place == index, row, 0.0)
+
+
+def sigmoid(value):
+    return 1.0 / (1.0 + jnp.exp(-value))
+
+
+def reduced(mail, here, part, stage, land, acc, between=None):
+    copies = []
+    for j in range(CHIPS):
+        value = part(j)
+        if j == 0:
+            acc[...] = value
+        else:
+            stage[j - 1] = value.astype(BF)
+            copies.append(mail.post(stage.at[j - 1], land.at[j - 1], here.peer(j)))
+    if between is not None:
+        between()
+    for copy in copies:
+        copy.wait_recv()
+    total = acc[...]
+    for j in range(1, CHIPS):
+        total = total + land[j - 1].astype(F32)
+    return total
+
+
+def feed_through(mail, here, hidden, keep, up, down, stage, land, acc, down_ready=None):
+    copies = spread(mail, here, hidden)
+    half = up[0].shape[1]
+
+    def part(j):
+        arrive(copies, j)
+        rows = hidden[j]
+        total = None
+        swishes = []
+        for side in range(2):
+            active = mm(rows, up[side][...])
+            keep[j, :, side * half : (side + 1) * half] = active
+            swishes.append((active * sigmoid(active)).astype(BF))
+        if j == 0 and down_ready is not None:
+            down_ready()
+        for side in range(2):
+            term = mm(swishes[side], down[side][...])
+            total = term if total is None else total + term
+        return total
+
+    return reduced(mail, here, part, stage, land, acc)
+
+
+def feed_return(mail, here, branch, hidden, keep, up, down, swish, active_grad, stage, land, acc, between):
+    copies = spread(mail, here, branch)
+    half = up[0].shape[1]
+
+    def part(j):
+        arrive(copies, j)
+        rows = branch[j]
+        total = None
+        for side in range(2):
+            span = slice(side * half, (side + 1) * half)
+            active = keep[j, :, span]
+            gate = sigmoid(active)
+            swish[j, :, span] = (active * gate).astype(BF)
+            grad = mm_right(rows, down[side][...]) * (gate * (1.0 + active * (1.0 - gate)))
+            grad = grad.astype(BF)
+            active_grad[j, :, span] = grad
+            term = mm_right(grad, up[side][...])
+            total = term if total is None else total + term
+        return total
+
+    return reduced(mail, here, part, stage, land, acc, between)
+
+
+def flat(ref, span=None):
+    value = ref[...] if span is None else ref[:, :, span]
+    return value.reshape(value.shape[0] * value.shape[1], value.shape[2])
+
+
+def feed_weight_grads(mail, here, branch, hidden, swish, active_grad, sums, up_out, down_out, pair):
+    half = swish.shape[2] // 2
+    up_send, up_land, down_send, down_land = pair
+    own, other = slice(0, half), slice(half, 2 * half)
+    branch_rows = flat(branch)
+    down_send[...] = mm_left(flat(swish, other), branch_rows).astype(BF)
+    down_copy = mail.post(down_send, down_land, here.sibling())
+    hidden_rows = flat(hidden)
+    up_send[...] = mm_left(hidden_rows, flat(active_grad, other)).astype(BF)
+    up_copy = mail.post(up_send, up_land, here.sibling())
+    sums[...] = mm_left(flat(swish, own), branch_rows)
+    down_copy.wait_recv()
+    value = (sums[...] + down_land[...].astype(F32)).astype(BF)
+    down_out[...] = value.reshape(down_out.shape)
+    grad = mm_left(hidden_rows, flat(active_grad, own))
+    up_copy.wait_recv()
+    by_owner(up_out, (grad + up_land[...].astype(F32)).astype(BF), here.planes)
+
+
+def by_owner(out, value, planes):
+    seqs = 2 * CHIPS
+    height = value.shape[0] // (seqs * planes)
+    for p in range(planes):
+        for s in range(seqs):
+            start = (s * planes + p) * height
+            out[p, s * height : (s + 1) * height, :] = value[start : start + height, :]
+
+
+def first_kernel(
+    planes, frames, small, up_src, down_src, qkv_src, out_src,
+    y_out, hidden, keep, up, down, small_out, qkv_out, out_out,
+    up_other, down_other, stage, land, acc, send, recv,
+):
+    here, mail = Here(planes), Mail(send, recv)
+    greet_near(here)
+    rows = frames.shape[1]
+    small_ready = over_planes(mail, here, small, lambda p: small_out.at[p])
+    up_height, qkv_height = up_src.shape[0], qkv_src.shape[0]
+    up_ready = over_planes(
+        mail, here, up_src,
+        lambda p: up.at[pl.ds(pl.multiple_of(p * up_height, up_height), up_height), :],
+    )
+    down_height = down.shape[0] // planes
+    down_own = down_src.at[pl.ds(pl.multiple_of(here.seq * down_height, down_height), down_height), :]
+    down_ready = over_planes(
+        mail, here, down_own,
+        lambda p: down.at[pl.ds(pl.multiple_of(p * down_height, down_height), down_height), :],
+    )
+    qkv_ready = over_planes(
+        mail, here, qkv_src,
+        lambda p: qkv_out.at[pl.ds(pl.multiple_of(p * qkv_height, qkv_height), qkv_height), :],
+    )
+    out_height = out_out.shape[0]
+    out_own = out_src.at[pl.ds(pl.multiple_of(here.core * out_height, out_height), out_height), :]
+    out_ready = from_plane(mail, here, out_own, out_out, here.chip)
+
+    value = frames[0].astype(F32)
+    white = whitened(value)[0]
+    small_ready()
+    hidden[0] = (white * scale_row(small_out, 0)).astype(BF)
+    up_ready()
+    up_copy = mail.post(up, up_other, here.sibling())
+    up_copy.wait_recv()
+
+    def both_down():
+        down_ready()
+        copy = mail.post(down, down_other, here.sibling())
+        copy.wait_recv()
+
+    total = feed_through(
+        mail, here, hidden, keep, (up, up_other), (down, down_other), stage, land, acc, both_down
+    )
+    y_out[...] = value + 0.5 * total
+    qkv_ready()
+    out_ready()
+    mail.close()
+
+
+def attention_weights(query, keys, slope, start, marks, row_ids):
+    height, width = query.shape[0], keys.shape[0]
+    row = lax.broadcasted_iota(jnp.int32, (height, width), 0) + start
+    column = lax.broadcasted_iota(jnp.int32, (height, width), 1)
+    distance = jnp.abs(row - column).astype(F32)
+    scores = mm_right(query, keys) * (1.0 / math.sqrt(query.shape[1])) - slope * distance
+    scores = jnp.where(marks[:, 6:7] == row_ids, scores, MASKED)
+    exponent = jnp.exp(scores - jnp.max(scores, axis=-1, keepdims=True))
+    return exponent / jnp.sum(exponent, axis=-1, keepdims=True), distance
+
+
+def attend_kernel(
+    planes, value_ref, small, qkv, out, slope, marks, row_ids, in_src, conv_src,
+    y_out, hidden, joint, mixed, in_out, conv_out,
+    qkv_other, out_other, joint_stage, mixed_stage, stage, land, acc, send, recv,
+):
+    here, mail = Here(planes), Mail(send, recv)
+    greet_near(here)
+    height = value_ref.shape[0]
+    size = joint.shape[1] // 3
+    weight_copies = [
+        mail.post(qkv, qkv_other, here.sibling()),
+        mail.post(out, out_other, here.sibling()),
+    ]
+    value = value_ref[...]
+    hidden[0] = (whitened(value)[0] * scale_row(small, 1)).astype(BF)
+    copies = spread(mail, here, hidden)
+    in_height = in_src.shape[0]
+    in_ready = over_planes(
+        mail, here, in_src,
+        lambda p: in_out.at[pl.ds(pl.multiple_of(p * in_height, in_height), in_height), :],
+    )
+    conv_height = conv_out.shape[0]
+    conv_own = conv_src.at[pl.ds(pl.multiple_of(here.core * conv_height, conv_height), conv_height), :]
+    conv_ready = from_plane(mail, here, conv_own, conv_out, here.chip)
+    for copy in weight_copies:
+        copy.wait_recv()
+    joint_copies = []
+    for j in range(CHIPS):
+        arrive(copies, j)
+        rows = hidden[j]
+        joint_stage[j] = mm(rows, qkv_other[...]).astype(BF)
+        joint_copies.append(
+            mail.post(joint_stage.at[j], joint.at[here.rows(j, height), :], here.sibling())
+        )
+        joint[here.rows(j, height), :] = mm(rows, qkv[...]).astype(BF)
+    for copy in joint_copies:
+        copy.wait_recv()
+    mixed_copies = []
+    for j in range(CHIPS):
+        start = pl.multiple_of(here.chips[j] * 2 * height, 2 * height)
+        block = pl.ds(start, 2 * height)
+        weights = attention_weights(
+            joint[block, 0:size], joint[:, size : 2 * size], slope[0], start, marks[block, :], row_ids[...]
+        )[0]
+        mixed_stage[j] = mm(weights.astype(BF), joint[:, 2 * size :]).astype(BF)
+        own = pl.ds(pl.multiple_of(here.core * height, height), height)
+        other = pl.ds(pl.multiple_of((1 - here.core) * height, height), height)
+        mixed[0, j] = mixed_stage[j, own, :]
+        mixed_copies.append(mail.post(mixed_stage.at[j, other, :], mixed.at[1, j], here.sibling()))
+
+    def part(j):
+        mixed_copies[j].wait_recv()
+        return mm(mixed[0, j], out[...]) + mm(mixed[1, j], out_other[...])
+
+    y_out[...] = value + reduced(mail, here, part, stage, land, acc)
+    in_ready()
+    conv_ready()
+    mail.close()
+
+
+def attend_back_kernel(
+    planes, grad_ref, value_ref, small, qkv, out, slope, marks, row_ids, hidden, joint, mixed, in_parts, conv_parts,
+    y_grad, small_grad, qkv_parts, out_parts, in_sum, conv_sum,
+    qkv_other, out_other, branch, mixed_stage, mixed_grad, joint_grad, key_grad, value_grad, moved,
+    qkv_send, qkv_land, out_send, out_land, in_land, conv_land, stage, land, acc, send, recv,
+):
+    here, mail = Here(planes), Mail(send, recv)
+    greet_near(here)
+    height = value_ref.shape[0]
+    size = joint.shape[1] // 3
+    weight_copies = [
+        mail.post(qkv, qkv_other, here.sibling()),
+        mail.post(out, out_other, here.sibling()),
+    ]
+    gradient = grad_ref[...]
+    branch[0] = gradient.astype(BF)
+    copies = spread(mail, here, branch)
+    in_total = sum_over_planes(mail, here, in_parts, in_land)
+    conv_total = sum_over_planes(mail, here, conv_parts, conv_land)
+    for copy in weight_copies:
+        copy.wait_recv()
+    mixed_copies = []
+    for j in range(CHIPS):
+        arrive(copies, j)
+        rows = branch[j]
+        mixed_stage[j] = mm_right(rows, out_other[...]).astype(BF)
+        mixed_copies.append(
+            mail.post(mixed_stage.at[j], mixed_grad.at[here.rows(j, height), :], here.sibling())
+        )
+        mixed_grad[here.rows(j, height), :] = mm_right(rows, out[...]).astype(BF)
+    for copy in mixed_copies:
+        copy.wait_recv()
+    key_grad[...] = jnp.zeros_like(key_grad)
+    value_grad[...] = jnp.zeros_like(value_grad)
+    scale = 1.0 / math.sqrt(size)
+
+    def step(index, carry):
+        start = pl.multiple_of(index * 2 * height, 2 * height)
+        block = pl.ds(start, 2 * height)
+        query, keys, values = joint[block, 0:size], joint[:, size : 2 * size], joint[:, 2 * size :]
+        weights, distance = attention_weights(query, keys, slope[0], start, marks[block, :], row_ids[...])
+        rows = mixed_grad[block, :]
+        weight_grad = mm_right(rows, values)
+        delta = jnp.sum(weights * weight_grad, axis=-1, keepdims=True)
+        score_grad = weights * (weight_grad - delta)
+        raw = (score_grad * scale).astype(BF)
+        joint_grad[block, 0:size] = mm(raw, keys).astype(BF)
+        key_grad[...] += mm_left(raw, query)
+        value_grad[...] += mm_left(weights.astype(BF), rows)
+        return carry - jnp.sum(score_grad * distance, axis=0, keepdims=True)
+
+    slope_row = lax.fori_loop(0, CHIPS, step, jnp.zeros((1, joint.shape[0]), F32))
+    joint_grad[:, size : 2 * size] = key_grad[...].astype(BF)
+    joint_grad[:, 2 * size :] = value_grad[...].astype(BF)
+    moved_copies = []
+    for j in range(CHIPS):
+        moved_copies.append(
+            mail.post(joint_grad.at[here.other_rows(j, height), :], moved.at[1, j], here.sibling())
+        )
+        moved[0, j] = joint_grad[here.rows(j, height), :]
+
+    def part(j):
+        moved_copies[j].wait_recv()
+        return mm_right(moved[0, j], qkv[...]) + mm_right(moved[1, j], qkv_other[...])
+
+    def between():
+        branch_rows = flat(branch)
+        out_send[...] = mm_left(flat(mixed.at[1]), branch_rows).astype(BF)
+        out_copy = mail.post(out_send, out_land, here.sibling())
+        hidden_rows = flat(hidden)
+        qkv_send[...] = mm_left(hidden_rows, flat(moved.at[1])).astype(BF)
+        qkv_copy = mail.post(qkv_send, qkv_land, here.sibling())
+        out_grad = mm_left(flat(mixed.at[0]), branch_rows)
+        out_copy.wait_recv()
+        out_parts[...] = (out_grad + out_land[...].astype(F32)).astype(BF).reshape(out_parts.shape)
+        qkv_grad = mm_left(hidden_rows, flat(moved.at[0]))
+        qkv_copy.wait_recv()
+        by_owner(qkv_parts, (qkv_grad + qkv_land[...].astype(F32)).astype(BF), here.planes)
+
+    total = reduced(mail, here, part, stage, land, acc, between)
+    value_part, gain_part = norm_grad(value_ref[...], scale_row(small, 1), total)
+    y_grad[...] = gradient + value_part
+    lane = lax.broadcasted_iota(jnp.int32, gain_part.shape, 1)
+    slope_total = jnp.sum(slope_row, axis=1, keepdims=True)
+    small_grad[...] = at_row(1, gain_part) + at_row(5, jnp.where(lane == here.seq, slope_total, 0.0))
+    in_sum[...] = in_total().astype(BF)
+    conv_sum[...] = conv_total()
+    mail.close()
+
+
+def conv_kernel(
+    planes, value_ref, small, conv_in, conv_out, marks, up_src, down_src,
+    y_out, hidden, joint, gated, standard, stats, mixed, up_out, down_out,
+    in_other, out_other, gate_stage, gate_rows, padded, mixed_rows, sums, sums_land, stage, land, acc, send, recv,
+):
+    here, mail = Here(planes), Mail(send, recv)
+    greet_near(here)
+    height = value_ref.shape[0]
+    width = gated.shape[1]
+    frames = gated.shape[0]
+    weight_copies = [
+        mail.post(conv_in, in_other, here.sibling()),
+        mail.post(conv_out, out_other, here.sibling()),
+    ]
+    value = value_ref[...]
+    hidden[0] = (whitened(value)[0] * scale_row(small, 2)).astype(BF)
+    copies = spread(mail, here, hidden)
+    up_height = up_src.shape[0]
+    up_ready = over_planes(
+        mail, here, up_src,
+        lambda p: up_out.at[pl.ds(pl.multiple_of(p * up_height, up_height), up_height), :],
+    )
+    down_height = down_out.shape[0] // planes
+    down_own = down_src.at[pl.ds(pl.multiple_of(here.seq * down_height, down_height), down_height), :]
+    down_ready = over_planes(
+        mail, here, down_own,
+        lambda p: down_out.at[pl.ds(pl.multiple_of(p * down_height, down_height), down_height), :],
+    )
+    for copy in weight_copies:
+        copy.wait_recv()
+    gate_copies = []
+    for j in range(CHIPS):
+        arrive(copies, j)
+        rows = hidden[j]
+        for side, weight in ((1, in_other), (0, conv_in)):
+            both = mm(rows, weight[...])
+            joint[j, :, 2 * width * side : 2 * width * (side + 1)] = both
+            gate = (both[:, :width] * sigmoid(both[:, width:])).astype(BF)
+            if side:
+                gate_stage[j] = gate
+                gate_copies.append(
+                    mail.post(gate_stage.at[j], gate_rows.at[here.rows(j, height), :], here.sibling())
+                )
+            else:
+                gate_rows[here.rows(j, height), :] = gate
+    for copy in gate_copies:
+        copy.wait_recv()
+    taps = 5
+    rim = 8
+    padded[0:rim, :] = jnp.zeros((rim, width), F32)
+    padded[rim + frames :, :] = jnp.zeros((rim, width), F32)
+    padded[rim : rim + frames, :] = gate_rows[...].astype(F32)
+    gated[...] = padded[rim : rim + frames, :]
+    kernel = own_channels(small, here, slice(5, 5 + taps), width)
+    conv = None
+    for t in range(taps):
+        first = rim - taps // 2 + t
+        term = kernel[t : t + 1, :] * padded[first : first + frames, :] * marks[:, t : t + 1]
+        conv = term if conv is None else conv + term
+    valid = marks[:, 5:6]
+    count = jnp.sum(valid, axis=0, keepdims=True)
+    total = jnp.sum(valid * conv, axis=0, keepdims=True)
+    centred = conv - total / count
+    squares = jnp.sum(valid * centred * centred, axis=0, keepdims=True)
+    sums[...] = at_row(0, total) + at_row(1, squares) + at_row(2, jnp.broadcast_to(count, total.shape))
+    sum_copies = [
+        mail.post(sums, sums_land.at[k - 1], here.above(k)) for k in range(1, planes)
+    ]
+    for copy in sum_copies:
+        copy.wait_recv()
+    terms = [sums[...]] + [sums_land[k - 1] for k in range(1, planes)]
+    whole = sum(term[2:3, :] for term in terms)
+    average = sum(term[0:1, :] for term in terms) / whole
+    variance = 0.0
+    for term in terms:
+        apart = term[0:1, :] / term[2:3, :] - average
+        variance = variance + term[1:2, :] + term[2:3, :] * apart * apart
+    inverse = lax.rsqrt(variance / whole + EPSILON)
+    stats[...] = at_row(0, inverse) + at_row(1, whole)
+    standard[...] = (conv - average) * inverse
+    scaled = standard[...] * own_channels(small, here, slice(10, 11), width)
+    mixed_rows[...] = (scaled * sigmoid(scaled)).astype(BF)
+    mixed_copies = []
+    for j in range(CHIPS):
+        mixed_copies.append(
+            mail.post(mixed_rows.at[here.other_rows(j, height), :], mixed.at[1, j], here.sibling())
+        )
+        mixed[0, j] = mixed_rows[here.rows(j, height), :]
+
+    def part(j):
+        mixed_copies[j].wait_recv()
+        return mm(mixed[0, j], conv_out[...]) + mm(mixed[1, j], out_other[...])
+
+    y_out[...] = value + reduced(mail, here, part, stage, land, acc)
+    up_ready()
+    down_ready()
+    mail.close()
+
+
+def conv_back_kernel(
+    planes, grad_ref, value_ref, small, conv_in, conv_out, marks, hidden, joint, gated, standard, stats, mixed,
+    up_parts, down_parts,
+    y_grad, small_grad, kernel_grad, cross, in_parts, out_parts, up_sum, down_sum,
+    in_other, out_other, branch, mixed_stage, mixed_grad, padded, gate_grad, moved, joint_grad, sums, sums_land,
+    in_send, in_land, out_send, out_land, up_land, down_land, stage, land, acc, send, recv,
+):
+    here, mail = Here(planes), Mail(send, recv)
+    greet_near(here)
+    height = value_ref.shape[0]
+    frames, width = gated.shape
+    weight_copies = [
+        mail.post(conv_out, out_other, here.sibling()),
+        mail.post(conv_in, in_other, here.sibling()),
+    ]
+    gradient = grad_ref[...]
+    branch[0] = gradient.astype(BF)
+    copies = spread(mail, here, branch)
+    up_total = sum_over_planes(mail, here, up_parts, up_land)
+    down_total = sum_over_planes(mail, here, down_parts, down_land)
+    for copy in weight_copies:
+        copy.wait_recv()
+    mixed_copies = []
+    for j in range(CHIPS):
+        arrive(copies, j)
+        rows = branch[j]
+        mixed_stage[j] = mm_right(rows, out_other[...])
+        mixed_copies.append(
+            mail.post(mixed_stage.at[j], mixed_grad.at[here.rows(j, height), :], here.sibling())
+        )
+        mixed_grad[here.rows(j, height), :] = mm_right(rows, conv_out[...])
+    for copy in mixed_copies:
+        copy.wait_recv()
+    gain = own_channels(small, here, slice(10, 11), width)
+    white = standard[...]
+    scaled = white * gain
+    gate = sigmoid(scaled)
+    scaled_grad = mixed_grad[...] * (gate * (1.0 + scaled * (1.0 - gate)))
+    sums[...] = at_row(0, jnp.sum(scaled_grad, axis=0, keepdims=True)) + at_row(
+        1, jnp.sum(scaled_grad * white, axis=0, keepdims=True)
+    )
+    sum_copies = [
+        mail.post(sums, sums_land.at[k - 1], here.above(k)) for k in range(1, planes)
+    ]
+    for copy in sum_copies:
+        copy.wait_recv()
+    both = sums[...]
+    for k in range(1, planes):
+        both = both + sums_land[k - 1]
+    cross[...] = both
+    inverse, whole = stats[0:1, :], stats[1:2, :]
+    conv_grad = inverse * (scaled_grad * gain) - marks[:, 5:6] * (
+        (inverse / whole) * (gain * both[0:1, :] + white * (gain * both[1:2, :]))
+    )
+    taps = 5
+    rim = 8
+    reach = taps // 2
+    padded[0:rim, :] = jnp.zeros((rim, width), F32)
+    padded[rim + frames :, :] = jnp.zeros((rim, width), F32)
+    padded[rim : rim + frames, :] = conv_grad
+    kernel = own_channels(small, here, slice(5, 5 + taps), width)
+    total = None
+    for t in range(taps):
+        first = rim + reach - t
+        mirror = taps - 1 - t
+        term = kernel[t : t + 1, :] * padded[first : first + frames, :] * marks[:, mirror : mirror + 1]
+        total = term if total is None else total + term
+    gate_grad[...] = total
+    moved_copies = []
+    for j in range(CHIPS):
+        moved_copies.append(
+            mail.post(gate_grad.at[here.other_rows(j, height), :], moved.at[1, j], here.sibling())
+        )
+        moved[0, j] = gate_grad[here.rows(j, height), :]
+
+    def part(j):
+        moved_copies[j].wait_recv()
+        result = None
+        for side, weight in ((0, conv_in), (1, in_other)):
+            left = joint[j, :, 2 * width * side : 2 * width * side + width]
+            gate = sigmoid(joint[j, :, 2 * width * side + width : 2 * width * (side + 1)])
+            incoming = moved[side, j]
+            joint_grad[side, j, :, :width] = (incoming * gate).astype(BF)
+            joint_grad[side, j, :, width:] = (incoming * left * (gate * (1.0 - gate))).astype(BF)
+            term = mm_right(joint_grad[side, j], weight[...])
+            result = term if result is None else result + term
+        return result
+
+    def between():
+        branch_rows = flat(branch)
+        out_send[...] = mm_left(flat(mixed.at[1]), branch_rows).astype(BF)
+        out_copy = mail.post(out_send, out_land, here.sibling())
+        hidden_rows = flat(hidden)
+        in_send[...] = mm_left(hidden_rows, flat(joint_grad.at[1])).astype(BF)
+        in_copy = mail.post(in_send, in_land, here.sibling())
+        out_grad = mm_left(flat(mixed.at[0]), branch_rows)
+        out_copy.wait_recv()
+        out_parts[...] = (out_grad + out_land[...].astype(F32)).astype(BF).reshape(out_parts.shape)
+        in_grad = mm_left(hidden_rows, flat(joint_grad.at[0]))
+        in_copy.wait_recv()
+        by_owner(in_parts, (in_grad + in_land[...].astype(F32)).astype(BF), here.planes)
+        dense = padded[rim : rim + frames, :]
+        padded[rim : rim + frames, :] = gated[...]
+        rows = jnp.zeros((8, width), F32)
+        for t in range(taps):
+            first = rim - reach + t
+            row = jnp.sum(padded[first : first + frames, :] * marks[:, t : t + 1] * dense, axis=0, keepdims=True)
+            rows = rows + at_row(t, row)
+        kernel_grad[...] = rows
+
+    whole_grad = reduced(mail, here, part, stage, land, acc, between)
+    value_part, gain_part = norm_grad(value_ref[...], scale_row(small, 2), whole_grad)
+    y_grad[...] = gradient + value_part
+    small_grad[...] = at_row(2, gain_part)
+    up_sum[...] = up_total().astype(BF)
+    down_sum[...] = down_total().astype(BF)
+    mail.close()
+
+
+def second_kernel(
+    planes, value_ref, small, up, down, out_grad,
+    result, y_grad, small_grad, up_parts, down_parts,
+    up_other, down_other, hidden, keep, branch, swish, active_grad,
+    stage, land, stage_back, land_back, acc, up_send, up_land, down_send, down_land, sums, send, recv,
+):
+    here, mail = Here(planes), Mail(send, recv)
+    greet_near(here)
+    weight_copies = [
+        mail.post(up, up_other, here.sibling()),
+        mail.post(down, down_other, here.sibling()),
+    ]
+    value = value_ref[...]
+    gain = scale_row(small, 3)
+    hidden[0] = (whitened(value)[0] * gain).astype(BF)
+    for copy in weight_copies:
+        copy.wait_recv()
+    ups, downs = (up, up_other), (down, down_other)
+    fourth = value + 0.5 * feed_through(mail, here, hidden, keep, ups, downs, stage, land, acc)
+    last_gain = scale_row(small, 4)
+    result[0] = (whitened(fourth)[0] * last_gain).astype(BF)
+    gradient, last_part = norm_grad(fourth, last_gain, out_grad[0].astype(F32))
+    branch[0] = (0.5 * gradient).astype(BF)
+
+    def between():
+        feed_weight_grads(
+            mail, here, branch, hidden, swish, active_grad, sums, up_parts, down_parts,
+            (up_send, up_land, down_send, down_land),
+        )
+
+    y_grad[...] = gradient
+    total = feed_return(
+        mail, here, branch, hidden, keep, ups, downs, swish, active_grad, stage_back, land_back, acc, between
+    )
+    value_part, gain_part = norm_grad(value_ref[...], gain, total)
+    y_grad[...] = y_grad[...] + value_part
+    small_grad[...] = at_row(3, gain_part) + at_row(4, last_part)
+    mail.close()
+
+
+def first_back_kernel(
+    planes, grad_ref, frames, small, up, down, hidden, keep, qkv_parts, out_parts,
+    x_grad, small_grad, up_parts, down_parts, qkv_sum, out_sum,
+    up_other, down_other, branch, swish, active_grad, qkv_land, out_land,
+    stage, land, acc, up_send, up_land, down_send, down_land, sums, send, recv,
+):
+    here, mail = Here(planes), Mail(send, recv)
+    greet_near(here)
+    weight_copies = [
+        mail.post(down, down_other, here.sibling()),
+        mail.post(up, up_other, here.sibling()),
+    ]
+    gradient = grad_ref[...]
+    branch[0] = (0.5 * gradient).astype(BF)
+    qkv_total = sum_over_planes(mail, here, qkv_parts, qkv_land)
+    out_total = sum_over_planes(mail, here, out_parts, out_land)
+    for copy in weight_copies:
+        copy.wait_recv()
+
+    def between():
+        feed_weight_grads(
+            mail, here, branch, hidden, swish, active_grad, sums, up_parts, down_parts,
+            (up_send, up_land, down_send, down_land),
+        )
+
+    total = feed_return(
+        mail, here, branch, hidden, keep, (up, up_other), (down, down_other), swish, active_grad, stage, land, acc, between
+    )
+    value_part, gain_part = norm_grad(frames[0].astype(F32), scale_row(small, 0), total)
+    x_grad[0] = grad_ref[...] + value_part
+    small_grad[...] = at_row(0, gain_part)
+    qkv_sum[...] = qkv_total().astype(BF)
+    out_sum[...] = out_total()
+    mail.close()
+
+
+def last_kernel(
+    planes, up_parts, down_parts, up_second, qkv_sum, in_sum, small_a, small_b, small_c, small_d, kernel_part,
+    up_first_out, up_second_out, qkv_out, in_out, down_out, small_out, kernel_out,
+    up_land, down_land, up_sum, up_got, second_got, qkv_got, in_got,
+    small_sum, small_land, small_near, kernel_land, send, recv,
+):
+    here, mail = Here(planes), Mail(send, recv)
+    near = [here.peer(j) for j in range(1, CHIPS)] + [here.cross(j) for j in range(CHIPS)]
+    greet(near + [here.above(k) for k in range(1, planes)])
+    up_total = sum_over_planes(mail, here, up_parts, up_land)
+    down_total = sum_over_planes(mail, here, down_parts, down_land)
+    small_sum[...] = small_a[...] + small_b[...] + small_c[...] + small_d[...]
+    small_copies = [mail.post(small_sum, small_land.at[k - 1], here.above(k)) for k in range(1, planes)]
+    kernel_copies = [mail.post(kernel_part, kernel_land.at[k - 1], here.above(k)) for k in range(1, planes)]
+    blocks = up_second_out.shape[0]
+    lane = 128
+
+    def swap(source, got):
+        return [
+            mail.post(
+                source.at[pl.ds(pl.multiple_of(device[0] * blocks, blocks), blocks), :], got.at[i], device
+            )
+            for i, device in enumerate(near)
+        ]
+
+    def place(source, got, out, copies):
+        stride = out.shape[1] // (source.shape[1] // lane)
+        own = source[pl.ds(pl.multiple_of(here.seq * blocks, blocks), blocks), :]
+        for i in range(len(near) + 1):
+            if i:
+                copies[i - 1].wait_recv()
+            seq = near[i - 1][0] if i else here.seq
+            value = (got[i - 1] if i else own).astype(F32)
+            for g in range(source.shape[1] // lane):
+                at = pl.ds(pl.multiple_of(g * stride + seq * lane, lane), lane)
+                out[:, at] = value[:, g * lane : (g + 1) * lane]
+
+    second_copies = swap(up_second, second_got)
+    qkv_copies = swap(qkv_sum, qkv_got)
+    in_copies = swap(in_sum, in_got)
+    for copy in small_copies:
+        copy.wait_recv()
+    total = small_sum[...]
+    for k in range(1, planes):
+        total = total + small_land[k - 1]
+    small_out[...] = total
+    near_copies = [mail.post(small_out, small_near.at[i], device) for i, device in enumerate(near)]
+    for copy in kernel_copies:
+        copy.wait_recv()
+    kernel_total = kernel_part[...]
+    for k in range(1, planes):
+        kernel_total = kernel_total + kernel_land[k - 1]
+    kernel_out[...] = kernel_total
+    up_sum[...] = up_total().astype(BF)
+    up_copies = swap(up_sum, up_got)
+    down_out[...] = down_total().astype(BF)
+    place(up_second, second_got, up_second_out, second_copies)
+    place(qkv_sum, qkv_got, qkv_out, qkv_copies)
+    place(in_sum, in_got, in_out, in_copies)
+    for copy in near_copies:
+        copy.wait_recv()
+    mail.close()
+    total = small_out[...]
+    for i in range(len(near)):
+        total = total + small_near[i]
+    small_out[...] = total
+    place(up_sum, up_got, up_first_out, up_copies)
+    mail.close()
+
+
+def launch(kernel, name, index, planes, operands, results, scratch):
+    spaces = {"v": pltpu.VMEM, "h": pl.ANY, "s": pltpu.SMEM}
+    return pl.pallas_call(
+        functools.partial(kernel, planes),
+        name=name,
+        out_shape=[jax.ShapeDtypeStruct(shape, kind) for shape, kind, _ in results],
+        in_specs=[pl.BlockSpec(memory_space=spaces[place]) for _, place in operands],
+        out_specs=[pl.BlockSpec(memory_space=spaces[place]) for _, _, place in results],
+        scratch_shapes=[pltpu.VMEM(shape, kind) for shape, kind in scratch]
+        + [pltpu.SemaphoreType.DMA((SLOTS,)), pltpu.SemaphoreType.DMA((SLOTS,))],
+        compiler_params=pltpu.CompilerParams(
+            collective_id=index, has_side_effects=True, vmem_limit_bytes=GRANT
+        ),
+    )(*[array for array, _ in operands])
+
+
+def pieces(weight, count, seq, width):
+    stride = weight.shape[1] // count
+    return jnp.concatenate(
+        [lax.dynamic_slice_in_dim(weight, g * stride + seq * width, width, axis=1) for g in range(count)],
+        axis=1,
+    )
+
+
+def plane_body(
+    frames, lengths, up_first, down_first, joint_qkv, attn_out, conv_in, conv_kernel_, batch_gain, conv_out,
+    up_second, down_second, norm_gains, slopes, out_grad,
+):
+    planes = lax.axis_size("fsdp")
+    seqs = lax.axis_size("seq")
+    seq = lax.axis_index("seq")
+    plane = lax.axis_index("fsdp")
+    rows, width = frames.shape[1], frames.shape[2]
+    length = rows * seqs
+    heads = slopes.shape[0]
+    size = width // heads
+    channels = width // seqs
+    hidden_units = up_first.shape[1]
+    half = hidden_units // seqs
+    shard = up_first.shape[0]
+    taps = conv_kernel_.shape[0]
+    block = width // (seqs * planes)
+    down_block = hidden_units // (seqs * planes)
+
+    bounds = jnp.cumsum(lengths[0])
+    positions = jnp.arange(length, dtype=jnp.int32)
+    ids = item_index(positions, bounds)
+    reach = taps // 2
+    rim_pos = positions[:, None] + jnp.arange(taps, dtype=jnp.int32)[None, :] - reach
+    rim_ids = jnp.sum((rim_pos[:, :, None] >= bounds[None, None, :]).astype(jnp.int32), axis=2)
+    shared = (rim_ids == ids[:, None]) & (rim_pos >= 0) & (rim_pos < length)
+    valid = ids < lengths.shape[1]
+    marks = jnp.concatenate(
+        [shared.astype(F32), valid.astype(F32)[:, None], ids.astype(F32)[:, None], jnp.zeros((length, 1), F32)],
+        axis=1,
+    )
+    row_ids = ids.astype(F32)[None, :]
+    slope = lax.dynamic_slice_in_dim(slopes, seq, 1)
+    small = jnp.concatenate(
+        [norm_gains, conv_kernel_, batch_gain[None, :], jnp.zeros((5, batch_gain.shape[0]), BF)], axis=0
+    )
+    up_piece = pieces(up_first, planes, seq, half // planes)
+    qkv_piece = pieces(joint_qkv, 3, seq, size)
+    in_piece = pieces(conv_in, 2, seq, channels)
+    second_piece = pieces(up_second, planes, seq, half // planes)
+
+    row_f = ((rows, width), F32, "v")
+    quad = (CHIPS, rows, width)
+    stage = ((CHIPS - 1, rows, width), BF)
+    acc = ((rows, width), F32)
+    tail = [stage, stage, acc]
+
+    first, hidden0, keep0, up1, down1, small_all, qkv, out_w = launch(
+        first_kernel, "first", 0, planes,
+        [(frames, "v"), (small, "v"), (up_piece, "h"), (down_first, "h"), (qkv_piece, "h"), (attn_out, "h")],
+        [
+            row_f, (quad, BF, "v"), ((CHIPS, rows, 2 * half), F32, "v"), ((width, half), BF, "v"),
+            ((half, width), BF, "v"), ((planes,) + small.shape, BF, "v"), ((width, 3 * size), BF, "h"),
+            ((size, width), BF, "h"),
+        ],
+        [((width, half), BF), ((half, width), BF)] + tail,
+    )
+    second, hidden1, joint, mixed, in_w, conv_w = launch(
+        attend_kernel, "attend", 1, planes,
+        [
+            (first, "v"), (small_all, "v"), (qkv, "v"), (out_w, "v"), (slope, "s"), (marks, "v"), (row_ids, "v"),
+            (in_piece, "h"), (conv_out, "h"),
+        ],
+        [
+            row_f, (quad, BF, "v"), ((length, 3 * size), BF, "v"), ((2, CHIPS, rows, size), BF, "v"),
+            ((width, 2 * channels), BF, "h"), ((channels, width), BF, "h"),
+        ],
+        [
+            ((width, 3 * size), BF), ((size, width), BF), ((CHIPS, rows, 3 * size), BF),
+            ((CHIPS, 2 * rows, size), BF),
+        ] + tail,
+    )
+    third, hidden2, glu, gated, standard, stats, swish, up2, down2 = launch(
+        conv_kernel, "conv", 2, planes,
+        [
+            (second, "v"), (small_all, "v"), (in_w, "v"), (conv_w, "v"), (marks, "v"), (second_piece, "h"),
+            (down_second, "h"),
+        ],
+        [
+            row_f, (quad, BF, "v"), ((CHIPS, rows, 4 * channels), F32, "v"), ((length, channels), F32, "v"),
+            ((length, channels), F32, "v"), ((8, channels), F32, "v"), ((2, CHIPS, rows, channels), BF, "v"),
+            ((width, half), BF, "h"), ((half, width), BF, "h"),
+        ],
+        [
+            ((width, 2 * channels), BF), ((channels, width), BF), ((CHIPS, rows, channels), BF),
+            ((length, channels), BF), ((length + 16, channels), F32), ((length, channels), BF),
+            ((8, channels), F32), ((planes - 1, 8, channels), F32),
+        ] + tail,
+    )
+    feed_scratch = [((width, half), BF), ((width, half), BF), ((half, width), BF), ((half, width), BF), ((half, width), F32)]
+    up_blocks = ((planes, width // planes, half), BF, "v")
+    down_blocks = ((planes, half // planes, width), BF, "v")
+    small_row = ((8, width), F32, "v")
+    result, third_grad, small_d, up2_parts, down2_parts = launch(
+        second_kernel, "second", 3, planes,
+        [(third, "v"), (small_all, "v"), (up2, "v"), (down2, "v"), (out_grad, "v")],
+        [((1, rows, width), BF, "v"), row_f, small_row, up_blocks, down_blocks],
+        [
+            ((width, half), BF), ((half, width), BF), (quad, BF), ((CHIPS, rows, 2 * half), F32), (quad, BF),
+            ((CHIPS, rows, 2 * half), BF), ((CHIPS, rows, 2 * half), BF), stage, stage, stage, stage, acc,
+        ] + feed_scratch,
+    )
+    second_grad, small_c, kernel_part, cross, in_parts, conv_parts, up2_sum, down2_sum = launch(
+        conv_back_kernel, "conv_back", 4, planes,
+        [
+            (third_grad, "v"), (second, "v"), (small_all, "v"), (in_w, "v"), (conv_w, "v"), (marks, "v"),
+            (hidden2, "v"), (glu, "v"), (gated, "v"), (standard, "v"), (stats, "v"), (swish, "v"),
+            (up2_parts, "v"), (down2_parts, "v"),
+        ],
+        [
+            row_f, small_row, ((8, channels), F32, "v"), ((8, channels), F32, "v"),
+            ((planes, width // planes, 2 * channels), BF, "v"), ((planes, channels // planes, width), BF, "v"),
+            ((width // planes, half), BF, "v"), ((half // planes, width), BF, "v"),
+        ],
+        [
+            ((width, 2 * channels), BF), ((channels, width), BF), (quad, BF), ((CHIPS, rows, channels), F32),
+            ((length, channels), F32), ((length + 16, channels), F32), ((length, channels), F32),
+            ((2, CHIPS, rows, channels), F32), ((2, CHIPS, rows, 2 * channels), BF), ((8, channels), F32),
+            ((planes - 1, 8, channels), F32), ((width, 2 * channels), BF), ((width, 2 * channels), BF),
+            ((channels, width), BF), ((channels, width), BF), ((planes - 1, width // planes, half), BF),
+            ((planes - 1, half // planes, width), BF),
+        ] + tail,
+    )
+    first_grad, small_b, qkv_parts, out_parts, in_sum, conv_out_grad = launch(
+        attend_back_kernel, "attend_back", 5, planes,
+        [
+            (second_grad, "v"), (first, "v"), (small_all, "v"), (qkv, "v"), (out_w, "v"), (slope, "s"), (marks, "v"),
+            (row_ids, "v"), (hidden1, "v"), (joint, "v"), (mixed, "v"), (in_parts, "v"), (conv_parts, "v"),
+        ],
+        [
+            row_f, small_row, ((planes, width // planes, 3 * size), BF, "v"),
+            ((planes, size // planes, width), BF, "v"), ((width // planes, 2 * channels), BF, "v"),
+            ((channels // planes, width), F32, "v"),
+        ],
+        [
+            ((width, 3 * size), BF), ((size, width), BF), (quad, BF), ((CHIPS, rows, size), BF),
+            ((length, size), BF), ((length, 3 * size), BF), ((length, size), F32), ((length, size), F32),
+            ((2, CHIPS, rows, 3 * size), BF), ((width, 3 * size), BF), ((width, 3 * size), BF),
+            ((size, width), BF), ((size, width), BF), ((planes - 1, width // planes, 2 * channels), BF),
+            ((planes - 1, channels // planes, width), BF),
+        ] + tail,
+    )
+    frames_grad, small_a, up1_parts, down1_parts, qkv_sum, attn_out_grad = launch(
+        first_back_kernel, "first_back", 6, planes,
+        [
+            (first_grad, "v"), (frames, "v"), (small_all, "v"), (up1, "v"), (down1, "v"), (hidden0, "v"),
+            (keep0, "v"), (qkv_parts, "v"), (out_parts, "v"),
+        ],
+        [
+            ((1, rows, width), F32, "v"), small_row, up_blocks, down_blocks,
+            ((width // planes, 3 * size), BF, "v"), ((size // planes, width), F32, "v"),
+        ],
+        [
+            ((width, half), BF), ((half, width), BF), (quad, BF), ((CHIPS, rows, 2 * half), BF),
+            ((CHIPS, rows, 2 * half), BF), ((planes - 1, width // planes, 3 * size), BF),
+            ((planes - 1, size // planes, width), BF),
+        ] + tail + feed_scratch,
+    )
+    near = seqs - 1
+    up1_grad, up2_grad, qkv_grad, in_grad, down1_sum, small_total, kernel_total = launch(
+        last_kernel, "last", 7, planes,
+        [
+            (up1_parts, "v"), (down1_parts, "v"), (up2_sum, "v"), (qkv_sum, "v"), (in_sum, "v"), (small_a, "v"),
+            (small_b, "v"), (small_c, "v"), (small_d, "v"), (kernel_part, "v"),
+        ],
+        [
+            ((block, hidden_units), F32, "v"), ((block, hidden_units), F32, "v"), ((block, 3 * width), F32, "v"),
+            ((block, 2 * width), F32, "v"), ((half // planes, width), BF, "v"), small_row,
+            ((8, channels), F32, "v"),
+        ],
+        [
+            ((planes - 1, width // planes, half), BF), ((planes - 1, half // planes, width), BF),
+            ((width // planes, half), BF), ((near, block, half), BF), ((near, block, half), BF),
+            ((near, block, 3 * size), BF), ((near, block, 2 * channels), BF), ((8, width), F32),
+            ((planes - 1, 8, width), F32), ((near, 8, width), F32), ((planes - 1, 8, channels), F32),
+        ],
+    )
+    total = seqs * planes
+    owners = []
+    for s in range(seqs):
+        for p in range(planes):
+            owners.append((s * planes + p, p * seqs + s))
+    down1_grad = lax.ppermute(down1_sum, ("seq", "fsdp"), owners).astype(F32)
+    down2_grad = lax.ppermute(down2_sum, ("seq", "fsdp"), owners).astype(F32)
+    place = seq * planes + plane
+    gains_grad = lax.dynamic_slice_in_dim(small_total, place * block, block, axis=1)[:5]
+    kernel_grad = lax.dynamic_slice_in_dim(kernel_total, plane * block, block, axis=1)[:taps]
+    batch_grad = lax.dynamic_slice_in_dim(cross[1], plane * block, block)
+    slopes_grad = small_total[5, :heads]
+    return (
+        result, frames_grad, up1_grad, down1_grad, qkv_grad, attn_out_grad, in_grad, kernel_grad, batch_grad,
+        conv_out_grad, up2_grad, down2_grad, gains_grad, slopes_grad,
+    )
+
+
 def solution(mesh):
+    planar = mesh.shape["seq"] == 2 * CHIPS and mesh.shape["fsdp"] == CHIPS
+    chosen = plane_body if planar else body
     placed = (
         P("fsdp", "seq", None),
         P("fsdp", None),
@@ -454,7 +1565,7 @@
         P("fsdp", "seq", None),
     )
     return jax.shard_map(
-        body,
+        chosen,
         mesh=mesh,
         in_specs=placed,
         out_specs=(

time: 3430 us -> 533 us (0.16)
  waiting for transfers between devices: 2960 us -> 9.58 us
  Pallas kernels: 0 us -> 483 us
  blocking collectives: 232 us -> 0 us
  matrix products: 141 us -> 0 us
    reduce_scatter x8 -> x0, waiting for transfers between devices: 2100 us -> none  [the longest x1 365 us: body(): lax.psum_scatter(second_up_grad, ('seq', 'fsdp'), scatter_dimension=0, ti...]
    all_gather x11 -> x0, waiting for transfers between devices: 746 us -> none  [the longest x1 145 us: body(): lax.all_gather(sharded[1], 'fsdp', axis=0, tiled=True)]
    pallas_call x0 -> x8, Pallas kernels: none -> 483 us  [launch(): pl.pallas_call(functools.partial(kernel, planes), name=name, out_shape=[j...]
    psum x4 -> x0, blocking collectives: 170 us -> none  [the longest x1 46.3 us: body(): lax.psum(jnp.sum(valid * centred * centred, axis=0), ('seq', 'fsdp'))]
    dot_general x31 -> x0, matrix products: 141 us -> none  [the longest x8 51.1 us: transposed_left(): lax.dot_general(left, right, (((0,), (0,)), ((), ())), preferred_element_...]
    unnamed x23 -> x0, waiting for transfers between devices: 108 us -> none
    all_gather x6 -> x0, blocking collectives: 62 us -> none  [the longest x1 13.4 us: body(): lax.all_gather(sharded[5], 'fsdp', axis=1, tiled=True)]
  transfers between devices with their start and end apart: 25 -> 2, of which waited for: 18 -> 1; matrix products, arithmetic and copies ran while one was open for 5% -> 1% of each run, Pallas kernels for 0% -> 28%
where the time goes in v1:
time: 533 us; the launch traced here: 524 us
  Pallas kernels  483 us (91%)
  local copies, waits for them, and re-layouts  17 us (3%)
  waiting for transfers between devices  9.58 us (2%)
  other arithmetic  6.34 us (1%)
  starting transfers between devices  6.28 us (1%)
    pallas_call x8, Pallas kernels, launch(): pl.pallas_call(functools.partial(kernel, planes), name=name, out_shape=[j...  483 us
  transfers between devices with their start and end apart: 2, of which 1 were waited for; matrix products, arithmetic and copies ran while one was open for 1% of the time, Pallas kernels for 28%

profile of v1, /device:TPU:4, one launch (start us, length us, event | category | flops | bytes accessed | tf_op | source)
XLA Modules:
  0.0 523.6 jit_solution(1151867351450089225)
XLA Ops:
  0.6 0.0 copy-start.10
  0.7 0.0 copy-start.9
  0.7 0.8 reduce-window.8
  1.5 0.1 convert_reduce_fusion.1
  1.6 0.0 copy-start.8
  1.6 0.7 broadcast_in_dim.6
  2.3 0.1 convert_reduce_fusion
  2.4 0.1 pad.9.clone
  2.5 0.1 maximum_maximum_fusion
  2.6 1.0 copy.36.marks
  3.6 1.2 dynamic_slice.60.slope
  4.8 0.1 pad.20.clone
  4.9 0.9 constant_dynamic-slice_fusion.8
  5.8 0.7 pad_maximum_fusion.3.in_src
  6.5 0.9 constant_dynamic-slice_fusion.11
  7.4 0.7 pad_maximum_fusion.2.qkv_src
  8.1 0.0 copy-done.10
  8.1 0.0 copy-done.9
  8.1 0.7 maximum_maximum_fusion.1.small
  8.8 1.1 constant_dynamic-slice_fusion.6
  9.9 0.7 pad_maximum_fusion.1.up_src
  10.6 0.7 pad_maximum_fusion.up_src
  11.4 0.0 copy-done.8
  11.4 81.2 %first.1 = (f32[128,1024]{1,0:T(8,128)}, bf16[4,128,1024]{2,1,0:T(8,128)(2,1)}, f32[4,128,1024]{2,1,0:T(8,128)}, bf16[1024,512]{1,0:T(8,128)(2,1)}, bf16[512,102...) custom-call(bf16[1,128,1024]{2,1,0:T(8,128)(2,1)} %frames.3, ...), custom_call_target="tpu_custom_call" | custom-call | tf_op jit(solution)/shard_map/first/pallas_call | solution.py:1329
  92.6 49.5 %attend.1 = (f32[128,1024]{1,0:T(8,128)}, bf16[4,128,1024]{2,1,0:T(8,128)(2,1)}, bf16[1024,384]{1,0:T(8,128)(2,1)}, bf16[2,4,128,128]{3,2,1,0:T(8,128)(2,1)}, bf...) custom-call(f32[128,1024]{1,0:T(8,128)} %get-tuple-element.69.value_ref, bf16[4,16,256]{2,1,0:T(8,128)(2,1)} %get-tuple-element.70.small, ...), custom_call_target="tpu_custom_call" | custom-call | tf_op jit(solution)/shard_map/attend/pallas_call | solution.py:1329
  142.1 70.6 %conv.1 = (f32[128,1024]{1,0:T(8,128)}, bf16[4,128,1024]{2,1,0:T(8,128)(2,1)}, f32[4,128,512]{2,1,0:T(8,128)}, f32[1024,128]{1,0:T(8,128)}, f32[1024,128]{1,0:T(...) custom-call(f32[128,1024]{1,0:T(8,128)} %get-tuple-element.73.value_, ...), custom_call_target="tpu_custom_call" | custom-call | tf_op jit(solution)/shard_map/conv/pallas_call | solution.py:1329
  212.6 62.8 %second.1 = (bf16[1,128,1024]{2,1,0:T(8,128)(2,1)}, f32[128,1024]{1,0:T(8,128)}, f32[8,1024]{1,0:T(8,128)}, bf16[4,256,512]{2,1,0:T(8,128)(2,1)}, bf16[4,128,1024]{2,1,0:T(8,128)(2,1)}) custom-call(f32[128,1024]{1,0:T(8,128)} %get-tuple-element.76.value_ref, bf16[4,16,256]{2,1,0:T(8,128)(2,1)} %get-tuple-element.70.small, ...), custom_call_target="tpu_custom_call" | custom-call | tf_op jit(solution)/shard_map/second/pallas_call | solution.py:1329
  275.4 70.8 %conv_back.1 = (f32[128,1024]{1,0:T(8,128)}, f32[8,1024]{1,0:T(8,128)}, f32[8,128]{1,0:T(8,128)}, f32[8,128]{1,0:T(8,128)}, bf16[4,256,256]{2,1,0:T(8,128)(2,1)}...) custom-call(f32[128,1024]{1,0:T(8,128)} %get-tuple-element.80.grad_ref, ...), custom_call_target="tpu_custom_call" | custom-call | tf_op jit(solution)/shard_map/conv_back/pallas_call | solution.py:1329
  346.2 3.8 collective-permute-start.1
  350.0 48.3 %attend_back.1 = (f32[128,1024]{1,0:T(8,128)}, f32[8,1024]{1,0:T(8,128)}, bf16[4,256,384]{2,1,0:T(8,128)(2,1)}, bf16[4,32,1024]{2,1,0:T(8,128)(2,1)}, bf16[256,256]{1,0:T(8,128)(2,1)}, /*index=5*/f32[32,1024]{1,0:T(8,128)}) custom-call(f32[128,1024]{1,0:T(8,128)} %get-tuple-element.89.grad_ref, f32[128,1024]{1,0:T(8,128)} %get-tuple-element.69.value_ref, ...), custom_call_target="tpu_custom_call" | custom-call | tf_op jit(solution)/shard_map/attend_back/pallas_call | solution.py:1329
  398.3 36.7 %first_back.1 = (f32[1,128,1024]{2,1,0:T(8,128)}, f32[8,1024]{1,0:T(8,128)}, bf16[4,256,512]{2,1,0:T(8,128)(2,1)}, bf16[4,128,1024]{2,1,0:T(8,128)(2,1)}, bf16[256,384]{1,0:T(8,128)(2,1)}, /*index=5*/f32[32,1024]{1,0:T(8,128)}) custom-call(f32[128,1024]{1,0:T(8,128)} %get-tuple-element.95.grad_ref, bf16[1,128,1024]{2,1,0:T(8,128)(2,1)} %frames.3, ...), custom_call_target="tpu_custom_call" | custom-call | tf_op jit(solution)/shard_map/first_back/pallas_call | solution.py:1329
  435.0 0.0 copy-start.4
  435.0 0.0 copy-start
  435.0 63.5 %last.1 = (f32[32,4096]{1,0:T(8,128)}, f32[32,4096]{1,0:T(8,128)}, f32[32,3072]{1,0:T(8,128)}, f32[32,2048]{1,0:T(8,128)}, bf16[128,1024]{1,0:T(8,128)(2,1)}, /*index=5*/f32[8,1024]{1,0:T(8,128)}, f32[8,128]{1,0:T(8,128)}) custom-call(bf16[4,256,512]{2,1,0:T(8,128)(2,1)} %get-tuple-element.103.up_parts, bf16[4,128,1024]{2,1,0:T(8,128)(2,1)} %get-tuple-element.104.down_parts, ...), custom_call_target="tpu_custom_call" | custom-call | tf_op jit(solution)/shard_map/last/pallas_call | solution.py:1329
  498.6 0.0 copy-start.2
  498.6 2.5 collective-permute-start
  501.1 0.7 slice.13
  501.8 1.3 constant_dynamic-slice_fusion
  503.1 1.3 constant_dynamic-slice_fusion.2
  504.5 0.6 fusion
  505.1 1.2 slice_bitcast_fusion
  506.2 0.0 copy-start.3
  506.2 0.0 collective-permute-done.1
  506.2 0.8 convert_element_type.61
  507.1 0.0 copy-start.7
  507.1 0.0 copy-start.5
  507.1 9.6 %collective-permute-done = bf16[128,1024]{1,0:T(8,128)(2,1)S(1)} collective-permute-done((bf16[128,1024]{1,0:T(8,128)(2,1)}, bf16[128,1024]{1,0:T(8,128)(2,1)S(1)}, u32[]{:S(2)}, u32[]{:S(2)}) %collective-permute-start) | collective-permute-done | bytes 262176 | tf_op jit(solution)/shard_map/ppermute | solution.py:1534
  516.7 0.8 convert_element_type.60
  517.5 0.0 copy-done.4
  517.5 0.7 copy.48
  518.2 0.0 copy-done
  518.2 0.8 copy.49
  519.0 0.0 copy-done.2
  519.0 0.8 copy.50
  519.8 0.0 copy-done.3
  519.8 0.7 copy.51
  520.6 0.0 copy-done.7
  520.6 0.7 copy.52
  521.2 0.0 copy-done.5
  521.2 0.7 copy.53
  521.9 0.0 copy-done.6
  521.9 0.7 copy.54
  522.6 0.0 copy-done.1
  522.6 0.8 copy.55
  (7 shorter events, 0.0 us)
Async XLA Ops:
  0.6 7.5 %copy-start.10 = (bf16[5,256]{1,0:T(8,128)(2,1)S(1)}, bf16[5,256]{1,0:T(8,128)(2,1)}, u32[]{:S(2)}) copy-start(bf16[5,256]{1,0:T(8,128)(2,1)} %param.27) | copy-start | bytes 7684
  0.7 7.5 %copy-start.9 = (bf16[5,256]{1,0:T(8,128)(2,1)S(1)}, bf16[5,256]{1,0:T(8,128)(2,1)}, u32[]{:S(2)}) copy-start(bf16[5,256]{1,0:T(8,128)(2,1)} %param.22) | copy-start | bytes 7684
  1.6 9.8 %copy-start.8 = (f32[1024]{0:T(1024)}, f32[1024]{0:T(1024)S(1)}, u32[]{:S(2)}) copy-start(f32[1024]{0:T(1024)S(1)} %convert_element_type.57) | copy-start | bytes 12292
  346.2 160.0 %collective-permute-start.1 = (bf16[128,1024]{1,0:T(8,128)(2,1)}, bf16[128,1024]{1,0:T(8,128)(2,1)S(1)}, u32[]{:S(2)}, u32[]{:S(2)}) collective-permute-start(bf16[128,1024]{1,0:T(8,128)(2,1)} %get-tuple-element.122), channel_id=1, source_target_pairs={{0,0},{1,8},{2,16},{3,24},{4,1},{5,9},{6,17},{7,25},{8,2},{9,10},{... | collective-permute-start | bytes 786440 | tf_op jit(solution)/shard_map/ppermute | solution.py:1535
  435.0 82.5 %copy-start.4 = (bf16[1,128,1024]{2,1,0:T(8,128)(2,1)S(1)}, bf16[1,128,1024]{2,1,0:T(8,128)(2,1)}, u32[]{:S(2)}) copy-start(bf16[1,128,1024]{2,1,0:T(8,128)(2,1)} %get-tuple-element.155) | copy-start | bytes 786436
  435.0 83.2 %copy-start = (f32[1,128,1024]{2,1,0:T(8,128)S(1)}, f32[1,128,1024]{2,1,0:T(8,128)}, u32[]{:S(2)}) copy-start(f32[1,128,1024]{2,1,0:T(8,128)} %get-tuple-element.156) | copy-start | bytes 1572868
  498.6 20.5 %copy-start.2 = (f32[32,4096]{1,0:T(8,128)S(1)}, f32[32,4096]{1,0:T(8,128)}, u32[]{:S(2)}) copy-start(f32[32,4096]{1,0:T(8,128)} %get-tuple-element.157) | copy-start | bytes 1572868
  498.6 18.1 %collective-permute-start = (bf16[128,1024]{1,0:T(8,128)(2,1)}, bf16[128,1024]{1,0:T(8,128)(2,1)S(1)}, u32[]{:S(2)}, u32[]{:S(2)}) collective-permute-start(bf16[128,1024]{1,0:T(8,128)(2,1)} %get-tuple-element.114), channel_id=1, source_target_pairs={{0,0},{1,8},{2,16},{3,24},{4,1},{5,9},{6,17},{7,25},{8,2},{9,10},{... | collective-permute-start | bytes 786440 | tf_op jit(solution)/shard_map/ppermute | solution.py:1534
  506.2 13.6 %copy-start.3 = (f32[32,3072]{1,0:T(8,128)S(1)}, f32[32,3072]{1,0:T(8,128)}, u32[]{:S(2)}) copy-start(f32[32,3072]{1,0:T(8,128)} %get-tuple-element.159) | copy-start | bytes 1179652
  507.1 13.5 %copy-start.7 = (f32[32,1024]{1,0:T(8,128)S(1)}, f32[32,1024]{1,0:T(8,128)}, u32[]{:S(2)}) copy-start(f32[32,1024]{1,0:T(8,128)} %get-tuple-element.160) | copy-start | bytes 393220
  507.1 14.1 %copy-start.5 = (f32[32,2048]{1,0:T(8,128)S(1)}, f32[32,2048]{1,0:T(8,128)}, u32[]{:S(2)}) copy-start(f32[32,2048]{1,0:T(8,128)} %get-tuple-element.161) | copy-start | bytes 786436
  517.5 4.4 copy-start.6
  518.2 4.4 copy-start.1
